TPU v7x, 32 devices: a whole 2x2x4 slice. The times are simulated.
32 devices in a mesh: band: 16 (over z, y, core), slab: 2 (over x).
Axes of the slice: x: 2, y: 2, z: 4, core: 2. Of those that a mesh axis runs over, the one named last changes fastest.
Arguments:
- orbitals: float32 [16, 160, 160, 160], P('band', 'slab'), may hold values from -6 to 6
Outputs:
- exchange_field: float32 [16, 160, 160, 160], P('band', 'slab')
All inputs are finite; a program needn't handle non-finite values.
Results may differ from a plain program's by a relative error of at most 0.0003.
Values sent between devices are 32-bit elements; how exact they have to be, the bound alone decides.
A program may use at most 192 MiB of HBM per device.

v0:
```python
import math

import jax
import jax.numpy as jnp
from jax import lax
from jax.sharding import PartitionSpec as P

STEPS = 2


highest = lax.Precision.HIGHEST


def passed_along(value, axis, steps):
    count = lax.axis_size(axis)
    pairs = [(source, (source + steps) % count) for source in range(count)]
    return lax.ppermute(value, axis, pairs)


def cas_table(length):
    indices = jnp.arange(length, dtype=jnp.int32)
    product = indices[:, None] * indices[None, :] % length
    phases = product.astype(jnp.float32) * (2.0 * math.pi / length)
    return jnp.cos(phases) + jnp.sin(phases)


def wave_square(indices, length):
    return 4.0 * jnp.sin(indices.astype(jnp.float32) * (math.pi / length)) ** 2


def potential(density, hartley, kernel, length):
    field = jnp.einsum("xk,zyx->zyk", hartley, density, precision=highest)
    field = jnp.einsum("yk,zyx->zkx", hartley, field, precision=highest)
    field = lax.all_to_all(field, "slab", split_axis=1, concat_axis=0, tiled=True)
    field = jnp.einsum("zk,zyx->kyx", hartley, field, precision=highest)
    field = field * kernel
    field = jnp.einsum("zk,zyx->kyx", hartley, field, precision=highest)
    field = jnp.einsum("xk,zyx->zyk", hartley, field, precision=highest)
    field = lax.all_to_all(field, "slab", split_axis=0, concat_axis=1, tiled=True)
    field = jnp.einsum("yk,zyx->zkx", hartley, field, precision=highest)
    return field / float(length**3)


def shards(orbitals):
    resident = orbitals[0]
    length = resident.shape[2]
    groups = lax.axis_size("slab")
    width_y = length // groups
    hartley = cas_table(length)
    waves = wave_square(jnp.arange(length, dtype=jnp.int32), length)
    first_y = lax.axis_index("slab") * width_y
    waves_y = wave_square(first_y + jnp.arange(width_y, dtype=jnp.int32), length)
    square = waves[:, None, None] + waves_y[None, :, None] + waves[None, None, :]
    kernel = jnp.where(square > 0, 1.0 / jnp.where(square > 0, square, 1.0), 0.0)
    accumulated = jnp.zeros(resident.shape, jnp.float32)
    visiting = passed_along(resident, "band", 1)
    travel_sum = jnp.zeros(resident.shape, jnp.float32)
    for offset in range(STEPS):
        if offset > 0:
            visiting, travel_sum = passed_along((visiting, travel_sum), "band", 1)
        field = potential(resident * visiting, hartley, kernel, length)
        accumulated = accumulated + field * visiting
        travel_sum = travel_sum + field * resident
    returned = passed_along(travel_sum, "band", -STEPS)
    accumulated = accumulated + returned
    return accumulated[None]


def solution(mesh):
    in_specs = (P("band", "slab", None, None),)
    out_specs = P("band", "slab", None, None)
    return jax.shard_map(shards, mesh=mesh, in_specs=in_specs, out_specs=out_specs, check_vma=False)
```

profile of v0, /device:TPU:1, one launch (start us, length us, event | category | flops | bytes accessed | tf_op | source)
XLA Modules:
  0.0 1350.9 jit_solution(3702766084560764651)
XLA Ops:
  0.0 15.3 %copy.30 = f32[1,80,160,160]{2,3,1,0:T(8,128)} copy(f32[1,80,160,160]{3,2,1,0:T(8,128)} %param.1) | data formatting | bytes 16384000 | tf_op args[0]
  17.9 141.3 %collective-permute-done = f32[80,160,160]{1,2,0:T(8,128)} collective-permute-done((f32[80,160,160]{1,2,0:T(8,128)}, f32[80,160,160]{1,2,0:T(8,128)}, u32[]{:S(2)}, u32[]{:S(2)}) %collective-permute-start) | collective-permute-done | bytes 8192032 | tf_op jit(solution)/shard_map/ppermute | solution.py:17
  159.2 21.6 %fusion.20 = f32[80,160,160]{1,2,0:T(8,128)} fusion(f32[80,160,160]{1,2,0:T(8,128)} %collective-permute-done, f32[1,80,160,160]{2,3,1,0:T(8,128)} %copy.30), kind=kOutput, calls=%fused_computation.26 | convolution fusion | flops 3934464000 | bytes 24576000 | tf_op jit(solution)/shard_map/xk,zyx->zyk/dot_general | solution.py:32
  180.8 17.2 %convolution_bitcast_fusion.1 = f32[80,160,160]{1,2,0:T(8,128)} fusion(f32[80,160,160]{1,2,0:T(8,128)} %fusion.20), kind=kOutput, calls=%fused_computation.29 | convolution fusion | flops 3932416000 | bytes 16384000 | tf_op jit(solution)/shard_map/yk,zyx->zkx/dot_general | solution.py:33
  198.0 15.5 %copy.33 = f32[80,160,160]{2,0,1:T(8,128)} copy(f32[80,160,160]{1,2,0:T(8,128)} %convolution_bitcast_fusion.1) | data formatting | bytes 16384000 | tf_op jit(solution)/shard_map/yk,zyx->zkx/transpose | solution.py:33
  213.5 8.6 all-to-all-start
  224.8 136.6 %all-to-all-done = f32[80,160,160]{2,0,1:T(8,128)} async-done(((f32[80,160,160]{2,0,1:T(8,128)}), f32[80,160,160]{2,0,1:T(8,128)}, u32[]{:S(2)}, u32[]{:S(2)}) %all-to-all-start) | async-done | bytes 8192032 | tf_op jit(solution)/shard_map/all_to_all | solution.py:34
  361.4 17.0 %copy.35 = f32[2,80,80,160]{3,2,1,0:T(8,128)} copy(f32[2,80,80,160]{3,1,2,0:T(8,128)} %bitcast.7) | data formatting | bytes 16384000 | tf_op jit(solution)/shard_map/all_to_all | solution.py:34
  378.4 22.1 %fusion.12 = f32[160,80,160]{2,0,1:T(8,128)S(1)} fusion(f32[160,80,160]{2,1,0:T(8,128)} %bitcast.89), kind=kOutput, calls=%fused_computation.18 | convolution fusion | flops 3932416000 | bytes 16384000 | tf_op jit(solution)/shard_map/zk,zyx->kyx/dot_general | solution.py:35
  400.6 18.2 %fusion.18 = f32[160,80,160]{2,0,1:T(8,128)} fusion(f32[160,80,160]{2,0,1:T(8,128)S(1)} %fusion.12, f32[160]{0:T(256)S(1)} %multiply_multiply_fusion, f32[160,80]{0,1:T(8,128)S(1)} %broadcast_add_fusion), kind=kOutput, calls=%fused_computation.24 | convolution fusion | flops 3944704000 | bytes 16435840 | tf_op jit(solution)/shard_map/zk,zyx->kyx/dot_general | solution.py:37
  418.7 25.3 %fusion.10 = f32[160,80,160]{2,1,0:T(8,128)} fusion(f32[160,80,160]{2,0,1:T(8,128)} %fusion.18), kind=kOutput, calls=%fused_computation.16 | convolution fusion | flops 3932416000 | bytes 16384000 | tf_op jit(solution)/shard_map/xk,zyx->zyk/dot_general | solution.py:38
  452.7 21.8 %fusion.16 = f32[80,160,160]{1,2,0:T(8,128)} fusion(f32[80,160,160]{1,2,0:T(8,128)} %collective-permute-done.1, f32[1,80,160,160]{2,3,1,0:T(8,128)} %copy.30), kind=kOutput, calls=%fused_computation.22 | convolution fusion | flops 3934464000 | bytes 24576000 | tf_op jit(solution)/shard_map/xk,zyx->zyk/dot_general | solution.py:32
  474.5 17.2 %convolution_bitcast_fusion = f32[80,160,160]{1,2,0:T(8,128)} fusion(f32[80,160,160]{1,2,0:T(8,128)} %fusion.16), kind=kOutput, calls=%fused_computation.28 | convolution fusion | flops 3932416000 | bytes 16384000 | tf_op jit(solution)/shard_map/yk,zyx->zkx/dot_general | solution.py:33
  491.7 15.7 %copy.43 = f32[80,160,160]{2,0,1:T(8,128)} copy(f32[80,160,160]{1,2,0:T(8,128)} %convolution_bitcast_fusion) | data formatting | bytes 16384000 | tf_op jit(solution)/shard_map/yk,zyx->zkx/transpose | solution.py:33
  507.4 83.6 %all-to-all-done.1 = f32[160,80,160]{2,1,0:T(8,128)} async-done(((f32[160,80,160]{2,1,0:T(8,128)}), f32[160,80,160]{2,1,0:T(8,128)}, u32[]{:S(2)}, u32[]{:S(2)}) %all-to-all-start.1) | async-done | bytes 8192032 | tf_op jit(solution)/shard_map/all_to_all | solution.py:39
  591.0 8.6 all-to-all-start.2
  599.7 21.4 %copy.40 = f32[80,2,80,160]{2,1,3,0:T(2,128)} copy(f32[80,2,80,160]{3,2,0,1:T(8,128)} %bitcast.10) | data formatting | bytes 16384000 | tf_op jit(solution)/shard_map/all_to_all | solution.py:39
  621.1 15.9 %all_to_all.59 = f32[80,160,160]{1,2,0:T(8,128)} reshape(f32[80,2,80,160]{2,1,3,0:T(2,128)} %copy.40) | data formatting | bytes 16384000 | tf_op jit(solution)/shard_map/all_to_all | solution.py:39
  637.0 25.0 %bitcast_multiply_fusion.2 = (f32[80,160,160]{1,2,0:T(8,128)}, f32[80,160,160]{2,1,0:T(8,128)}) fusion(f32[1,80,160,160]{2,3,1,0:T(8,128)} %copy.30, f32[80,160,160]{1,2,0:T(8,128)} %all_to_all.59), kind=kOutput, calls=%fused_computation.10 | convolution fusion | flops 3936512000 | bytes 32768000 | tf_op jit(solution)/shard_map/yk,zyx->zkx/dot_general | solution.py:40
  662.0 9.1 collective-permute-start.2
  671.1 66.1 %all-to-all-done.2 = f32[80,160,160]{2,0,1:T(8,128)} async-done(((f32[80,160,160]{2,0,1:T(8,128)}), f32[80,160,160]{2,0,1:T(8,128)}, u32[]{:S(2)}, u32[]{:S(2)}) %all-to-all-start.2) | async-done | bytes 8192032 | tf_op jit(solution)/shard_map/all_to_all | solution.py:34
  737.1 17.0 %copy.45 = f32[2,80,80,160]{3,2,1,0:T(8,128)} copy(f32[2,80,80,160]{3,1,2,0:T(8,128)} %bitcast.17) | data formatting | bytes 16384000 | tf_op jit(solution)/shard_map/all_to_all | solution.py:34
  754.2 22.4 %fusion.8 = f32[160,80,160]{2,0,1:T(8,128)S(1)} fusion(f32[160,80,160]{2,1,0:T(8,128)} %bitcast.90), kind=kOutput, calls=%fused_computation.14 | convolution fusion | flops 3932416000 | bytes 16384000 | tf_op jit(solution)/shard_map/zk,zyx->kyx/dot_general | solution.py:35
  776.6 17.9 %fusion.14 = f32[160,80,160]{2,0,1:T(8,128)} fusion(f32[160,80,160]{2,0,1:T(8,128)S(1)} %fusion.8, f32[160]{0:T(256)S(1)} %multiply_multiply_fusion, f32[160,80]{0,1:T(8,128)S(1)} %broadcast_add_fusion), kind=kOutput, calls=%fused_computation.20 | convolution fusion | flops 3944704000 | bytes 16435840 | tf_op jit(solution)/shard_map/zk,zyx->kyx/dot_general | solution.py:37
  794.5 23.3 %fusion.6 = f32[160,80,160]{2,1,0:T(8,128)S(1)} fusion(f32[160,80,160]{2,0,1:T(8,128)} %fusion.14), kind=kOutput, calls=%fused_computation.12 | convolution fusion | flops 3932416000 | bytes 16384000 | tf_op jit(solution)/shard_map/xk,zyx->zyk/dot_general | solution.py:38
  817.8 141.8 %all_to_all.72 = f32[160,80,160]{2,1,0:T(8,128)} all-to-all(f32[160,80,160]{2,1,0:T(8,128)S(1)} %fusion.6), channel_id=1, replica_groups=mesh['band'=16,'slab'=2] {'slab'}, dimensions={0} | all-to-all | bytes 16384000 | tf_op jit(solution)/shard_map/all_to_all | solution.py:39
  959.6 21.5 %copy.50 = f32[80,2,80,160]{2,1,3,0:T(2,128)} copy(f32[80,2,80,160]{3,2,0,1:T(8,128)} %bitcast.91) | data formatting | bytes 16384000 | tf_op jit(solution)/shard_map/all_to_all | solution.py:39
  981.1 16.2 %all_to_all.67 = f32[80,160,160]{1,2,0:T(8,128)} reshape(f32[80,2,80,160]{2,1,3,0:T(2,128)} %copy.50) | data formatting | bytes 16384000 | tf_op jit(solution)/shard_map/all_to_all | solution.py:39
  997.3 27.7 %fusion.5 = (f32[80,160,160]{1,2,0:T(8,128)}, f32[80,160,160]{2,1,0:T(8,128)}) fusion(f32[80,160,160]{1,2,0:T(8,128)} %collective-permute-done.2, f32[1,80,160,160]{2,3,1,0:T(8,128)} %copy.30, f32[80,160,160]{1,2,0:T(8,128)} %all_to_all.67), kind=kOutput, calls=%fused_computation.9 | convolution fusion | flops 3938560000 | bytes 40960000 | tf_op jit(solution)/shard_map/yk,zyx->zkx/dot_general | solution.py:40
  1030.1 282.3 %collective-permute-done.3 = f32[80,160,160]{1,2,0:T(8,128)S(1)} collective-permute-done((f32[80,160,160]{1,2,0:T(8,128)}, f32[80,160,160]{1,2,0:T(8,128)S(1)}, u32[]{:S(2)}, u32[]{:S(2)}) %collective-permute-start.3) | collective-permute-done | bytes 8192032 | tf_op jit(solution)/shard_map/ppermute | solution.py:17
  1312.3 22.9 %fusion.4 = f32[1,80,160,160]{2,3,1,0:T(8,128)} fusion(f32[80,160,160]{1,2,0:T(8,128)S(1)} %collective-permute-done.3, f32[80,160,160]{1,2,0:T(8,128)} %collective-permute-done.1, f32[80,160,160]{1,2,0:T(8,128)} %collective-permute-done, f32[80,160,160]{2,1,0:T(8,128)} %get-tuple-element.8, f32[80,160,160]{2,1,0:T(8,128)} %get-tuple-element.6), kind=kLoop, calls=%fused_computation.8 | loop fusion | flops 12288000 | bytes 49152000 | tf_op jit(solution)/shard_map/broadcast_in_dim | solution.py:66
  1335.2 15.3 %copy.51 = f32[1,80,160,160]{3,2,1,0:T(8,128)} copy(f32[1,80,160,160]{2,3,1,0:T(8,128)} %fusion.4) | data formatting | bytes 16384000 | tf_op jit(solution)/shard_map/broadcast_in_dim | solution.py:66
  (9 shorter events, 19.0 us)
Async XLA Ops:
  15.3 143.9 %collective-permute-start = (f32[80,160,160]{1,2,0:T(8,128)}, f32[80,160,160]{1,2,0:T(8,128)}, u32[]{:S(2)}, u32[]{:S(2)}) collective-permute-start(f32[80,160,160]{1,2,0:T(8,128)} %bitcast.88), channel_id=1, source_target_pairs={{0,2},{2,4},{4,6},{6,8},{8,10},{10,12},{12,14},{14,16},{16,18},{18... | collective-permute-start | bytes 24576008 | tf_op jit(solution)/shard_map/ppermute | solution.py:17
  213.5 147.9 %all-to-all-start = ((f32[80,160,160]{2,0,1:T(8,128)}), f32[80,160,160]{2,0,1:T(8,128)}, u32[]{:S(2)}, u32[]{:S(2)}) async-start(f32[80,160,160]{2,0,1:T(8,128)} %copy.33), calls=%async_computation | async-start | bytes 26214400 | tf_op jit(solution)/shard_map/all_to_all | solution.py:34
  222.1 230.6 %collective-permute-start.1 = (f32[80,160,160]{1,2,0:T(8,128)}, f32[80,160,160]{1,2,0:T(8,128)}, u32[]{:S(2)}, u32[]{:S(2)}) collective-permute-start(f32[80,160,160]{1,2,0:T(8,128)} %collective-permute-done), channel_id=1, source_target_pairs={{0,2},{2,4},{4,6},{6,8},{8,10},{10,12},{12,14},{14,16},{16,18},{18... | collective-permute-start | bytes 24576008 | tf_op jit(solution)/shard_map/ppermute | solution.py:17
  444.1 146.9 %all-to-all-start.1 = ((f32[160,80,160]{2,1,0:T(8,128)}), f32[160,80,160]{2,1,0:T(8,128)}, u32[]{:S(2)}, u32[]{:S(2)}) async-start(f32[160,80,160]{2,1,0:T(8,128)} %fusion.10), calls=%async_computation.1 | async-start | bytes 26214400 | tf_op jit(solution)/shard_map/all_to_all | solution.py:39
  591.0 146.1 %all-to-all-start.2 = ((f32[80,160,160]{2,0,1:T(8,128)}), f32[80,160,160]{2,0,1:T(8,128)}, u32[]{:S(2)}, u32[]{:S(2)}) async-start(f32[80,160,160]{2,0,1:T(8,128)} %copy.43), calls=%async_computation.2 | async-start | bytes 26214400 | tf_op jit(solution)/shard_map/all_to_all | solution.py:34
  662.0 335.3 %collective-permute-start.2 = (f32[80,160,160]{1,2,0:T(8,128)}, f32[80,160,160]{1,2,0:T(8,128)}, u32[]{:S(2)}, u32[]{:S(2)}) collective-permute-start(f32[80,160,160]{1,2,0:T(8,128)} %get-tuple-element.5), channel_id=1, source_target_pairs={{0,2},{2,4},{4,6},{6,8},{8,10},{10,12},{12,14},{14,16},{16,18},{18... | collective-permute-start | bytes 24576008 | tf_op jit(solution)/shard_map/ppermute | solution.py:17
  1025.0 287.4 %collective-permute-start.3 = (f32[80,160,160]{1,2,0:T(8,128)}, f32[80,160,160]{1,2,0:T(8,128)S(1)}, u32[]{:S(2)}, u32[]{:S(2)}) collective-permute-start(f32[80,160,160]{1,2,0:T(8,128)} %get-tuple-element.7), channel_id=1, source_target_pairs={{0,28},{2,30},{4,0},{6,2},{8,4},{10,6},{12,8},{14,10},{16,12},{18,... | collective-permute-start | bytes 24576008 | tf_op jit(solution)/shard_map/ppermute | solution.py:17
where the time goes:
time: 1370 us; the launch traced here: 1350 us
  waiting for transfers between devices  710 us (52%)
  matrix products  260 us (19%)
  local copies, waits for them, and re-layouts  171 us (12%)
  blocking collectives  142 us (10%)
  starting transfers between devices  45.1 us (3%)
  other arithmetic  23 us (2%)
    ppermute x4, waiting for transfers between devices, passed_along(): return lax.ppermute(value, axis, pairs)  424 us
    all_to_all x2, waiting for transfers between devices, potential(): lax.all_to_all(field, 'slab', split_axis=1, concat_axis=0, tiled=True)  203 us
    all_to_all x1, blocking collectives, potential(): lax.all_to_all(field, 'slab', split_axis=0, concat_axis=1, tiled=True)  142 us
    dot_general x4, matrix products, potential(): field = jnp.einsum('yk,zyx->zkx', hartley, field, precision=highest)  87.1 us
    all_to_all x1, waiting for transfers between devices, potential(): lax.all_to_all(field, 'slab', split_axis=0, concat_axis=1, tiled=True)  83.6 us
    dot_general x4, matrix products, potential(): field = jnp.einsum('zk,zyx->kyx', hartley, field, precision=highest)  80.7 us
    all_to_all x4, local copies, waits for them, and re-layouts, potential(): lax.all_to_all(field, 'slab', split_axis=0, concat_axis=1, tiled=True)  75 us
    dot_general x2, matrix products, potential(): field = jnp.einsum('xk,zyx->zyk', hartley, field, precision=highest)  48.6 us
  transfers between devices with their start and end apart: 7, of which 5 were waited for; matrix products, arithmetic and copies ran while one was open for 21% of the time, Pallas kernels for 0%

commit v1 on v0

v1 whole, which is shorter than its diff:
```python
import functools
import math

import jax
import jax.numpy as jnp
from jax import lax
from jax.experimental import pallas as pl
from jax.experimental.pallas import tpu as pltpu
from jax.sharding import PartitionSpec as P

CHUNKS = 4

high = lax.Precision.HIGH


def passed_along(value, axis, steps):
    count = lax.axis_size(axis)
    pairs = [(source, (source + steps) % count) for source in range(count)]
    return lax.ppermute(value, axis, pairs)


def cas_table(rows, columns, length):
    product = rows[:, None] * columns[None, :] % length
    phases = product.astype(jnp.float32) * (2.0 * math.pi / length)
    return jnp.cos(phases) + jnp.sin(phases)


def wave_square(indices, length):
    return 4.0 * jnp.sin(indices.astype(jnp.float32) * (math.pi / length)) ** 2


def halves(value):
    upper = value.astype(jnp.bfloat16)
    lower = (value - upper.astype(jnp.float32)).astype(jnp.bfloat16)
    return upper, lower


def table_halves(table):
    upper = lax.reduce_precision(table, exponent_bits=8, mantissa_bits=7)
    return upper.astype(jnp.bfloat16), (table - upper).astype(jnp.bfloat16)


def product3(left, right):
    dot = functools.partial(jnp.dot, preferred_element_type=jnp.float32)
    return dot(left[0], right[0]) + (dot(left[0], right[1]) + dot(left[1], right[0]))


def plane_transform(field, along_x, along_y):
    planes, rows, columns = field.shape
    flat = field.reshape(planes * rows, columns)
    flat = product3(halves(flat), along_x)
    split = halves(flat)
    out = []
    for plane in range(planes):
        part = slice(plane * rows, (plane + 1) * rows)
        out.append(product3(along_y, (split[0][part], split[1][part])))
    return out


def forward_kernel(a_ref, b_ref, xu_ref, xl_ref, yu_ref, yl_ref, *out_refs):
    density = a_ref[...] * b_ref[...]
    out = plane_transform(density, (xu_ref[...], xl_ref[...]), (yu_ref[...], yl_ref[...]))
    width = out_refs[0].shape[1]
    for plane, value in enumerate(out):
        for group, out_ref in enumerate(out_refs):
            out_ref[plane] = value[group * width : (group + 1) * width]


def inverse_kernel(groups, adds, *refs):
    pieces, refs = refs[:groups], refs[groups:]
    xu_ref, xl_ref, yu_ref, yl_ref, a_ref, b_ref = refs[:6]
    extra, (home_ref, away_ref) = refs[6:-2], refs[-2:]
    field = jnp.concatenate([piece[...] for piece in pieces], axis=1)
    out = plane_transform(field, (xu_ref[...], xl_ref[...]), (yu_ref[...], yl_ref[...]))
    for plane, value in enumerate(out):
        home = value * b_ref[plane]
        away = value * a_ref[plane]
        if adds:
            home = home + extra[0][plane]
            away = away + extra[1][plane]
        home_ref[plane] = home
        away_ref[plane] = away


def plane_block(depth):
    return max(size for size in range(1, 6) if depth % size == 0)


def plane_cost(depth, length, arrays):
    return pl.CostEstimate(
        flops=12 * depth * length**3,
        bytes_accessed=4 * arrays * depth * length**2,
        transcendentals=0,
    )


params = pltpu.CompilerParams(vmem_limit_bytes=40 * 1024 * 1024)


def forward(resident, start, visiting, tables_x, tables_y, groups):
    depth, length, _ = visiting.shape
    width = length // groups
    block = plane_block(depth)
    first = start // block
    table = pl.BlockSpec((length, length), lambda i: (0, 0))
    return pl.pallas_call(
        forward_kernel,
        grid=(depth // block,),
        in_specs=[
            pl.BlockSpec((block, length, length), lambda i: (first + i, 0, 0)),
            pl.BlockSpec((block, length, length), lambda i: (i, 0, 0)),
        ]
        + [table] * 4,
        out_specs=[pl.BlockSpec((block, width, length), lambda i: (i, 0, 0))] * groups,
        out_shape=[jax.ShapeDtypeStruct((depth, width, length), jnp.float32)] * groups,
        cost_estimate=plane_cost(depth, length, 3),
        compiler_params=params,
        name="forward",
    )(resident, visiting, *tables_x, *tables_y)


def inverse(pieces, tables_x, tables_y, resident, start, visiting, extra=()):
    groups = len(pieces)
    depth, length, _ = visiting.shape
    width = length // groups
    block = plane_block(depth)
    first = start // block
    table = pl.BlockSpec((length, length), lambda i: (0, 0))
    whole = pl.BlockSpec((block, length, length), lambda i: (i, 0, 0))
    shape = jax.ShapeDtypeStruct((depth, length, length), jnp.float32)
    return pl.pallas_call(
        functools.partial(inverse_kernel, groups, bool(extra)),
        grid=(depth // block,),
        in_specs=[pl.BlockSpec((block, width, length), lambda i: (i, 0, 0))] * groups
        + [table] * 4
        + [pl.BlockSpec((block, length, length), lambda i: (first + i, 0, 0)), whole]
        + [whole] * len(extra),
        out_specs=[whole] * 2,
        out_shape=[shape] * 2,
        cost_estimate=plane_cost(depth, length, 5 + len(extra)),
        compiler_params=params,
        name="inverse",
    )(*pieces, *tables_x, *tables_y, resident, visiting, *extra)


def shards(orbitals):
    resident = orbitals[0]
    local, _, length = resident.shape
    groups = lax.axis_size("slab")
    me = lax.axis_index("slab")
    width = length // groups
    depth = local // CHUNKS
    starts = [chunk * depth for chunk in range(CHUNKS)]
    grid = jnp.arange(length, dtype=jnp.int32)
    turned = (me * width + grid) % length
    table_x = table_halves(cas_table(grid, grid, length))
    table_y = table_halves(cas_table(turned, grid, length))
    back_y = table_halves(cas_table(grid, turned, length))
    order = jnp.concatenate(
        [(me - j) % groups * local + jnp.arange(local, dtype=jnp.int32) for j in range(groups)]
    )
    table_z = cas_table(grid, order, length)
    waves = wave_square(grid, length)
    waves_y = wave_square(me * width + jnp.arange(width, dtype=jnp.int32), length)
    square = waves[:, None, None] + waves_y[None, :, None] + waves[None, None, :]
    kernel = jnp.where(square > 0, 1.0 / jnp.where(square > 0, square, 1.0), 0.0)
    kernel = kernel / float(length**3)

    def spread(visiting):
        sent = []
        for chunk, start in enumerate(starts):
            parts = forward(resident, start, visiting[chunk], table_x, table_y, groups)
            sent.append(
                [parts[0]] + [passed_along(parts[j], "slab", j) for j in range(1, groups)]
            )
        return [sent[chunk][j] for j in range(groups) for chunk in range(CHUNKS)]

    def filtered(parts):
        field = jnp.concatenate(parts, axis=0)
        field = jnp.einsum("kz,zyx->kyx", table_z, field, precision=high)
        field = field * kernel
        return jnp.einsum("kz,kyx->zyx", table_z, field, precision=high)

    def gathered(field, start):
        parts = []
        for j in range(groups):
            part = field[j * local + start : j * local + start + depth]
            parts.append(passed_along(part, "slab", -j) if j else part)
        return parts

    near = [passed_along(resident[s : s + depth], "band", 1) for s in starts]
    far = [passed_along(part, "band", 1) for part in near]
    near_parts = spread(near)
    far_parts = spread(far)
    far_field = filtered(far_parts)
    near_field = filtered(near_parts)
    carried = []
    for chunk, start in enumerate(starts):
        parts = gathered(far_field, start)
        home, away = inverse(parts, table_x, back_y, resident, start, far[chunk])
        carried.append((home, passed_along(away, "band", -1)))
    out = []
    for chunk, start in enumerate(starts):
        parts = gathered(near_field, start)
        home, away = inverse(
            parts, table_x, back_y, resident, start, near[chunk], carried[chunk]
        )
        out.append(home + passed_along(away, "band", -1))
    return jnp.concatenate(out, axis=0)[None]


def solution(mesh):
    in_specs = (P("band", "slab", None, None),)
    out_specs = P("band", "slab", None, None)
    return jax.shard_map(shards, mesh=mesh, in_specs=in_specs, out_specs=out_specs, check_vma=False)
```

time: 1370 us -> 817 us (0.60)
  waiting for transfers between devices: 710 us -> 429 us
  matrix products: 260 us -> 86.6 us
  blocking collectives: 142 us -> 0 us
  Pallas kernels: 0 us -> 128 us
  local copies, waits for them, and re-layouts: 171 us -> 90.1 us
  starting transfers between devices: 45.1 us -> 61.4 us
    all_to_all x3 -> x0, waiting for transfers between devices: 286 us -> none  [the longest x2 203 us: potential(): lax.all_to_all(field, 'slab', split_axis=1, concat_axis=0, tiled=True)]
    dot_general x12 -> x4, matrix products: 260 us -> 86.6 us  [the longest x2 55.4 us: filtered(): field = jnp.einsum('kz,zyx->kyx', table_z, field, precision=high)]
    all_to_all x1 -> x0, blocking collectives: 142 us -> none  [potential(): lax.all_to_all(field, 'slab', split_axis=0, concat_axis=1, tiled=True)]
    pallas_call x0 -> x16, Pallas kernels: none -> 128 us  [the longest x8 68 us: inverse(): pl.pallas_call(functools.partial(inverse_kernel, groups, bool(extra)), gr...]
    all_to_all x6 -> x0, local copies, waits for them, and re-layouts: 109 us -> none  [the longest x4 75 us: potential(): lax.all_to_all(field, 'slab', split_axis=0, concat_axis=1, tiled=True)]
    ppermute x4 -> x32, starting transfers between devices: 19.3 us -> 61.4 us  [passed_along(): return lax.ppermute(value, axis, pairs)]
    unnamed x1 -> x118, local copies, waits for them, and re-layouts: 15.3 us -> 57.1 us
    slice x0 -> x3, local copies, waits for them, and re-layouts: none -> 31.6 us  [the longest x2 21.5 us: gathered(): part = field[j * local + start:j * local + start + depth]]
  transfers between devices with their start and end apart: 7 -> 32, of which waited for: 5 -> 18; matrix products, arithmetic and copies ran while one was open for 21% -> 13% of each run, Pallas kernels for 0% -> 16%
where the time goes in v1:
time: 817 us; the launch traced here: 807 us
  waiting for transfers between devices  429 us (53%)
  Pallas kernels  128 us (16%)
  local copies, waits for them, and re-layouts  90.1 us (11%)
  matrix products  86.6 us (11%)
  starting transfers between devices  61.4 us (8%)
  other arithmetic  11.9 us (1%)
    ppermute x32, waiting for transfers between devices, passed_along(): return lax.ppermute(value, axis, pairs)  429 us
    pallas_call x8, Pallas kernels, inverse(): pl.pallas_call(functools.partial(inverse_kernel, groups, bool(extra)), gr...  68 us
    ppermute x32, starting transfers between devices, passed_along(): return lax.ppermute(value, axis, pairs)  61.4 us
    pallas_call x8, Pallas kernels, forward(): pl.pallas_call(forward_kernel, grid=(depth // block,), in_specs=[pl.Block...  59.7 us
    unnamed x118, local copies, waits for them, and re-layouts  57.1 us
    dot_general x2, matrix products, filtered(): field = jnp.einsum('kz,zyx->kyx', table_z, field, precision=high)  55.4 us
    dot_general x2, matrix products, filtered(): return jnp.einsum('kz,kyx->zyx', table_z, field, precision=high)  31.2 us
    slice x2, local copies, waits for them, and re-layouts, gathered(): part = field[j * local + start:j * local + start + depth]  21.5 us
  transfers between devices with their start and end apart: 32, of which 18 were waited for; matrix products, arithmetic and copies ran while one was open for 13% of the time, Pallas kernels for 16%

profile of v1, /device:TPU:1, one launch (start us, length us, event | category | flops | bytes accessed | tf_op | source)
XLA Modules:
  0.0 807.2 jit_solution(4457764026301139300)
XLA Ops:
  0.0 10.1 %slice_bitcast_fusion = (f32[20,160,160]{2,1,0:T(8,128)}, f32[20,160,160]{2,1,0:T(8,128)}, f32[20,160,160]{2,1,0:T(8,128)}, f32[20,160,160]{2,1,0:T(8,128)}) fusion(f32[1,80,160,160]{3,2,1,0:T(8,128)} %param.1), kind=kLoop, calls=%fused_computation.14 | loop fusion | bytes 16384000 | tf_op jit(solution)/shard_map/slice | solution.py:191
  17.3 31.4 %collective-permute-done.b_ref.refs_7_ = f32[20,160,160]{2,1,0:T(8,128)} collective-permute-done((f32[20,160,160]{2,1,0:T(8,128)}, f32[20,160,160]{2,1,0:T(8,128)}, u32[]{:S(2)}, u32[]{:S(2)}) %collective-permute-start) | collective-permute-done | bytes 2048032 | tf_op jit(solution)/shard_map/ppermute | solution.py:19
  58.9 24.9 %collective-permute-done.1.b_ref.refs_7_ = f32[20,160,160]{2,1,0:T(8,128)} collective-permute-done((f32[20,160,160]{2,1,0:T(8,128)}, f32[20,160,160]{2,1,0:T(8,128)}, u32[]{:S(2)}, u32[]{:S(2)}) %collective-permute-start.1) | collective-permute-done | bytes 2048032 | tf_op jit(solution)/shard_map/ppermute | solution.py:19
  96.8 22.1 %collective-permute-done.2.b_ref.refs_7_ = f32[20,160,160]{2,1,0:T(8,128)} collective-permute-done((f32[20,160,160]{2,1,0:T(8,128)}, f32[20,160,160]{2,1,0:T(8,128)}, u32[]{:S(2)}, u32[]{:S(2)}) %collective-permute-start.2) | collective-permute-done | bytes 2048032 | tf_op jit(solution)/shard_map/ppermute | solution.py:19
  130.0 24.0 %collective-permute-done.3.b_ref.refs_7_ = f32[20,160,160]{2,1,0:T(8,128)S(1)} collective-permute-done((f32[20,160,160]{2,1,0:T(8,128)}, f32[20,160,160]{2,1,0:T(8,128)S(1)}, u32[]{:S(2)}, u32[]{:S(2)}) %collective-permute-start.3) | collective-permute-done | bytes 2048032 | tf_op jit(solution)/shard_map/ppermute | solution.py:19
  171.6 28.8 %collective-permute-done.7 = f32[20,80,160]{2,1,0:T(8,128)S(1)} collective-permute-done((f32[20,80,160]{2,1,0:T(8,128)S(1)}, f32[20,80,160]{2,1,0:T(8,128)S(1)}, u32[]{:S(2)}, u32[]{:S(2)}) %collective-permute-start.7) | collective-permute-done | bytes 1024032 | tf_op jit(solution)/shard_map/ppermute | solution.py:19
  213.7 10.5 %collective-permute-done.10.b_ref.refs_7_ = f32[20,160,160]{2,1,0:T(8,128)S(1)} collective-permute-done((f32[20,160,160]{2,1,0:T(8,128)}, f32[20,160,160]{2,1,0:T(8,128)S(1)}, u32[]{:S(2)}, u32[]{:S(2)}) %collective-permute-start.10) | collective-permute-done | bytes 2048032 | tf_op jit(solution)/shard_map/ppermute | solution.py:19
  224.2 8.0 forward.13
  233.5 25.8 %collective-permute-done.11.b_ref.refs_7_ = f32[20,160,160]{2,1,0:T(8,128)S(1)} collective-permute-done((f32[20,160,160]{2,1,0:T(8,128)}, f32[20,160,160]{2,1,0:T(8,128)S(1)}, u32[]{:S(2)}, u32[]{:S(2)}) %collective-permute-start.11) | collective-permute-done | bytes 2048032 | tf_op jit(solution)/shard_map/ppermute | solution.py:19
  269.4 32.7 %fusion.5 = f32[160,80,160]{2,0,1:T(8,128)} fusion(f32[160,80,160]{2,1,0:T(8,128)} %copy-done.35, s32[160]{0:T(256)S(1)} %pad_add_fusion), kind=kOutput, calls=%fused_computation.8 | convolution fusion | flops 1966336000 | bytes 16384640 | tf_op jit(solution)/shard_map/kz,zyx->kyx/dot_general | solution.py:180
  321.8 32.3 %collective-permute-done.16 = f32[20,80,160]{2,1,0:T(8,128)S(1)} collective-permute-done((f32[20,80,160]{2,1,0:T(8,128)S(1)}, f32[20,80,160]{2,1,0:T(8,128)S(1)}, u32[]{:S(2)}, u32[]{:S(2)}) %collective-permute-start.16) | collective-permute-done | bytes 1024032 | tf_op jit(solution)/shard_map/ppermute | solution.py:19
  355.3 22.8 %fusion.3 = f32[160,80,160]{2,0,1:T(8,128)} fusion(f32[160,80,160]{2,1,0:T(8,128)} %constant_dynamic-update-slice_fusion.8, s32[160]{0:T(256)S(1)} %pad_add_fusion), kind=kOutput, calls=%fused_computation.6 | convolution fusion | flops 1966336000 | bytes 16384640 | tf_op jit(solution)/shard_map/kz,zyx->kyx/dot_general | solution.py:180
  378.1 15.4 %fusion.7 = f32[160,80,160]{2,0,1:T(8,128)} fusion(f32[160,80,160]{2,0,1:T(8,128)} %fusion.3, f32[160]{0:T(256)S(1)} %multiply_multiply_fusion, f32[160,80]{0,1:T(8,128)S(1)} %broadcast_add_fusion, s32[160]{0:T(256)S(1)} %pad_add_fusion), kind=kOutput, calls=%fused_computation.10 | convolution fusion | flops 1980672000 | bytes 16436480 | tf_op jit(solution)/shard_map/kz,kyx->zyx/dot_general | solution.py:182
  393.5 10.0 %fusion.58 = (f32[20,80,160]{2,0,1:T(8,128)S(1)}, f32[20,80,160]{2,0,1:T(8,128)}, f32[20,80,160]{2,0,1:T(8,128)S(1)}, f32[20,80,160]{2,0,1:T(8,128)}, f32[20,80,...) fusion(f32[160,80,160]{2,0,1:T(8,128)} %fusion.7), kind=kLoop, calls=%fused_computation.104 | loop fusion | bytes 16384000 | tf_op jit(solution)/shard_map/slice | solution.py:187
  405.5 15.8 %fusion.9 = f32[160,80,160]{2,0,1:T(8,128)} fusion(f32[160,80,160]{2,0,1:T(8,128)} %fusion.5, f32[160]{0:T(256)S(1)} %multiply_multiply_fusion, f32[160,80]{0,1:T(8,128)S(1)} %broadcast_add_fusion, s32[160]{0:T(256)S(1)} %pad_add_fusion), kind=kOutput, calls=%fused_computation.12 | convolution fusion | flops 1980672000 | bytes 16436480 | tf_op jit(solution)/shard_map/kz,kyx->zyx/dot_general | solution.py:182
  426.1 11.5 %fusion.59 = (f32[20,80,160]{2,0,1:T(8,128)}, f32[20,80,160]{2,0,1:T(8,128)S(1)}, f32[20,80,160]{2,0,1:T(8,128)}, f32[20,80,160]{2,0,1:T(8,128)}, f32[20,80,160]...) fusion(f32[160,80,160]{2,0,1:T(8,128)} %fusion.9), kind=kLoop, calls=%fused_computation.105 | loop fusion | bytes 16384000 | tf_op jit(solution)/shard_map/slice | solution.py:187
  460.8 14.5 %collective-permute-done.21.refs_1_ = f32[20,80,160]{2,1,0:T(8,128)} collective-permute-done((f32[20,80,160]{2,1,0:T(8,128)}, f32[20,80,160]{2,1,0:T(8,128)}, u32[]{:S(2)}, u32[]{:S(2)}) %collective-permute-start.21) | collective-permute-done | bytes 1024032 | tf_op jit(solution)/shard_map/ppermute | solution.py:19
  475.3 7.9 inverse.10
  492.2 18.3 %collective-permute-done.25.refs_1_ = f32[20,80,160]{2,1,0:T(8,128)} collective-permute-done((f32[20,80,160]{2,1,0:T(8,128)}, f32[20,80,160]{2,1,0:T(8,128)}, u32[]{:S(2)}, u32[]{:S(2)}) %collective-permute-start.25) | collective-permute-done | bytes 1024032 | tf_op jit(solution)/shard_map/ppermute | solution.py:19
  510.4 7.9 inverse.12
  520.0 60.6 %collective-permute-done.29.refs_1_ = f32[20,80,160]{2,1,0:T(8,128)} collective-permute-done((f32[20,80,160]{2,1,0:T(8,128)}, f32[20,80,160]{2,1,0:T(8,128)}, u32[]{:S(2)}, u32[]{:S(2)}) %collective-permute-start.29) | collective-permute-done | bytes 1024032 | tf_op jit(solution)/shard_map/ppermute | solution.py:19
  587.9 8.0 inverse.14
  598.1 17.5 %collective-permute-done.20.refs_1_ = f32[20,80,160]{2,1,0:T(8,128)S(1)} collective-permute-done((f32[20,80,160]{2,1,0:T(8,128)}, f32[20,80,160]{2,1,0:T(8,128)S(1)}, u32[]{:S(2)}, u32[]{:S(2)}) %collective-permute-start.20) | collective-permute-done | bytes 1024032 | tf_op jit(solution)/shard_map/ppermute | solution.py:19
  621.5 9.7 %inverse.9 = (f32[20,160,160]{2,1,0:T(8,128)S(1)}, f32[20,160,160]{2,1,0:T(8,128)}) custom-call(f32[20,80,160]{2,1,0:T(8,128)S(1)} %copy.26.refs_0_, f32[20,80,160]{2,1,0:T(8,128)} %collective-permute-done.8.refs_1_, bf16[160,160]{1,0:T(8,128)(2,1)S(1)} %get-tuple-element.93.xu_ref.refs_2_, bf16[160,160]{1,0:T(8,128)(2,1)S(1)} %get-tuple-element.94.xl_ref.refs_3_, ...), custom_call_target="tpu_custom_call" | custom-call | flops 983040000 | bytes 14336000 | tf_op jit(solution)/shard_map/inverse/pallas_call | solution.py:131
  637.2 9.3 %inverse.11 = (f32[20,160,160]{2,1,0:T(8,128)S(1)}, f32[20,160,160]{2,1,0:T(8,128)}) custom-call(f32[20,80,160]{2,1,0:T(8,128)S(1)} %copy.30.refs_0_, f32[20,80,160]{2,1,0:T(8,128)S(1)} %copy-done.22, bf16[160,160]{1,0:T(8,128)(2,1)S(1)} %get-tuple-element.93.xu_ref.refs_2_, bf16[160,160]{1,0:T(8,128)(2,1)S(1)} %get-tuple-element.94.xl_ref.refs_3_, ...), custom_call_target="tpu_custom_call" | custom-call | flops 983040000 | bytes 14336000 | tf_op jit(solution)/shard_map/inverse/pallas_call | solution.py:131
  650.0 8.4 %collective-permute-start.23 = (f32[20,160,160]{2,1,0:T(8,128)}, f32[20,160,160]{2,1,0:T(8,128)S(1)}, u32[]{:S(2)}, u32[]{:S(2)}) collective-permute-start(f32[20,160,160]{2,1,0:T(8,128)} %get-tuple-element.60), channel_id=1, source_target_pairs={{0,30},{2,0},{4,2},{6,4},{8,6},{10,8},{12,10},{14,12},{16,14},{18,... | collective-permute-start | bytes 6144008 | tf_op jit(solution)/shard_map/ppermute | solution.py:19
  658.4 9.6 %inverse.13 = (f32[20,160,160]{2,1,0:T(8,128)S(1)}, f32[20,160,160]{2,1,0:T(8,128)}) custom-call(f32[20,80,160]{2,1,0:T(8,128)S(1)} %copy.34.refs_0_, f32[20,80,160]{2,1,0:T(8,128)} %collective-permute-done.24.refs_1_, bf16[160,160]{1,0:T(8,128)(2,1)S(1)} %get-tuple-element.93.xu_ref.refs_2_, bf16[160,160]{1,0:T(8,128)(2,1)S(1)} %get-tuple-element.94.xl_ref.refs_3_, ...), custom_call_target="tpu_custom_call" | custom-call | flops 983040000 | bytes 14336000 | tf_op jit(solution)/shard_map/inverse/pallas_call | solution.py:131
  669.7 15.4 %collective-permute-done.28.refs_1_ = f32[20,80,160]{2,1,0:T(8,128)} collective-permute-done((f32[20,80,160]{2,1,0:T(8,128)}, f32[20,80,160]{2,1,0:T(8,128)}, u32[]{:S(2)}, u32[]{:S(2)}) %collective-permute-start.28) | collective-permute-done | bytes 1024032 | tf_op jit(solution)/shard_map/ppermute | solution.py:19
  685.1 7.9 inverse.15
  697.9 33.3 %collective-permute-done.23 = f32[20,160,160]{2,1,0:T(8,128)S(1)} collective-permute-done((f32[20,160,160]{2,1,0:T(8,128)}, f32[20,160,160]{2,1,0:T(8,128)S(1)}, u32[]{:S(2)}, u32[]{:S(2)}) %collective-permute-start.23) | collective-permute-done | bytes 2048032 | tf_op jit(solution)/shard_map/ppermute | solution.py:19
  731.6 34.8 %collective-permute-done.27 = f32[20,160,160]{2,1,0:T(8,128)} collective-permute-done((f32[20,160,160]{2,1,0:T(8,128)}, f32[20,160,160]{2,1,0:T(8,128)}, u32[]{:S(2)}, u32[]{:S(2)}) %collective-permute-start.27) | collective-permute-done | bytes 2048032 | tf_op jit(solution)/shard_map/ppermute | solution.py:19
  768.8 32.6 %collective-permute-done.31 = f32[20,160,160]{2,1,0:T(8,128)S(1)} collective-permute-done((f32[20,160,160]{2,1,0:T(8,128)S(1)}, f32[20,160,160]{2,1,0:T(8,128)S(1)}, u32[]{:S(2)}, u32[]{:S(2)}) %collective-permute-start.31) | collective-permute-done | bytes 2048032 | tf_op jit(solution)/shard_map/ppermute | solution.py:19
  (188 shorter events, 184.7 us)
Async XLA Ops:
  10.1 38.6 %collective-permute-start = (f32[20,160,160]{2,1,0:T(8,128)}, f32[20,160,160]{2,1,0:T(8,128)}, u32[]{:S(2)}, u32[]{:S(2)}) collective-permute-start(f32[20,160,160]{2,1,0:T(8,128)} %get-tuple-element.87), channel_id=1, source_target_pairs={{0,2},{2,4},{4,6},{6,8},{8,10},{10,12},{12,14},{14,16},{16,18},{18... | collective-permute-start | bytes 6144008 | tf_op jit(solution)/shard_map/ppermute | solution.py:19
  12.7 71.0 %collective-permute-start.1 = (f32[20,160,160]{2,1,0:T(8,128)}, f32[20,160,160]{2,1,0:T(8,128)}, u32[]{:S(2)}, u32[]{:S(2)}) collective-permute-start(f32[20,160,160]{2,1,0:T(8,128)} %get-tuple-element.86), channel_id=1, source_target_pairs={{0,2},{2,4},{4,6},{6,8},{8,10},{10,12},{12,14},{14,16},{16,18},{18... | collective-permute-start | bytes 6144008 | tf_op jit(solution)/shard_map/ppermute | solution.py:19
  12.8 106.1 %collective-permute-start.2 = (f32[20,160,160]{2,1,0:T(8,128)}, f32[20,160,160]{2,1,0:T(8,128)}, u32[]{:S(2)}, u32[]{:S(2)}) collective-permute-start(f32[20,160,160]{2,1,0:T(8,128)} %get-tuple-element.88), channel_id=1, source_target_pairs={{0,2},{2,4},{4,6},{6,8},{8,10},{10,12},{12,14},{14,16},{16,18},{18... | collective-permute-start | bytes 6144008 | tf_op jit(solution)/shard_map/ppermute | solution.py:19
  14.4 139.6 %collective-permute-start.3 = (f32[20,160,160]{2,1,0:T(8,128)}, f32[20,160,160]{2,1,0:T(8,128)S(1)}, u32[]{:S(2)}, u32[]{:S(2)}) collective-permute-start(f32[20,160,160]{2,1,0:T(8,128)} %get-tuple-element.85), channel_id=1, source_target_pairs={{0,2},{2,4},{4,6},{6,8},{8,10},{10,12},{12,14},{14,16},{16,18},{18... | collective-permute-start | bytes 6144008 | tf_op jit(solution)/shard_map/ppermute | solution.py:19
  57.7 98.8 %collective-permute-start.4 = (f32[20,80,160]{2,1,0:T(8,128)}, f32[20,80,160]{2,1,0:T(8,128)}, u32[]{:S(2)}, u32[]{:S(2)}) collective-permute-start(f32[20,80,160]{2,1,0:T(8,128)} %get-tuple-element.41), channel_id=1, source_target_pairs={{0,1},{1,0},{2,3},{3,2},{4,5},{5,4},{6,7},{7,6},{8,9},{9,8},{10,11... | collective-permute-start | bytes 3072008 | tf_op jit(solution)/shard_map/ppermute | solution.py:19
  92.8 70.7 %collective-permute-start.5 = (f32[20,80,160]{2,1,0:T(8,128)}, f32[20,80,160]{2,1,0:T(8,128)}, u32[]{:S(2)}, u32[]{:S(2)}) collective-permute-start(f32[20,80,160]{2,1,0:T(8,128)} %get-tuple-element.42), channel_id=1, source_target_pairs={{0,1},{1,0},{2,3},{3,2},{4,5},{5,4},{6,7},{7,6},{8,9},{9,8},{10,11... | collective-permute-start | bytes 3072008 | tf_op jit(solution)/shard_map/ppermute | solution.py:19
  94.0 111.5 %collective-permute-start.9 = (f32[20,160,160]{2,1,0:T(8,128)}, f32[20,160,160]{2,1,0:T(8,128)S(1)}, u32[]{:S(2)}, u32[]{:S(2)}) collective-permute-start(f32[20,160,160]{2,1,0:T(8,128)} %collective-permute-done.b_ref.refs_7_), channel_id=1, source_target_pairs={{0,2},{2,4},{4,6},{6,8},{8,10},{10,12},{12,14},{14,16},{16,18},{18... | collective-permute-start | bytes 6144008 | tf_op jit(solution)/shard_map/ppermute | solution.py:19
  128.8 36.2 %collective-permute-start.6 = (f32[20,80,160]{2,1,0:T(8,128)S(1)}, f32[20,80,160]{2,1,0:T(8,128)S(1)}, u32[]{:S(2)}, u32[]{:S(2)}) collective-permute-start(f32[20,80,160]{2,1,0:T(8,128)S(1)} %get-tuple-element.43), channel_id=1, source_target_pairs={{0,1},{1,0},{2,3},{3,2},{4,5},{5,4},{6,7},{7,6},{8,9},{9,8},{10,11... | collective-permute-start | bytes 3072008 | tf_op jit(solution)/shard_map/ppermute | solution.py:19
  154.0 70.2 %collective-permute-start.10 = (f32[20,160,160]{2,1,0:T(8,128)}, f32[20,160,160]{2,1,0:T(8,128)S(1)}, u32[]{:S(2)}, u32[]{:S(2)}) collective-permute-start(f32[20,160,160]{2,1,0:T(8,128)} %collective-permute-done.1.b_ref.refs_7_), channel_id=1, source_target_pairs={{0,2},{2,4},{4,6},{6,8},{8,10},{10,12},{12,14},{14,16},{16,18},{18... | collective-permute-start | bytes 6144008 | tf_op jit(solution)/shard_map/ppermute | solution.py:19
  156.4 102.9 %collective-permute-start.11 = (f32[20,160,160]{2,1,0:T(8,128)}, f32[20,160,160]{2,1,0:T(8,128)S(1)}, u32[]{:S(2)}, u32[]{:S(2)}) collective-permute-start(f32[20,160,160]{2,1,0:T(8,128)} %collective-permute-done.2.b_ref.refs_7_), channel_id=1, source_target_pairs={{0,2},{2,4},{4,6},{6,8},{8,10},{10,12},{12,14},{14,16},{16,18},{18... | collective-permute-start | bytes 6144008 | tf_op jit(solution)/shard_map/ppermute | solution.py:19
  163.5 36.9 %collective-permute-start.7 = (f32[20,80,160]{2,1,0:T(8,128)S(1)}, f32[20,80,160]{2,1,0:T(8,128)S(1)}, u32[]{:S(2)}, u32[]{:S(2)}) collective-permute-start(f32[20,80,160]{2,1,0:T(8,128)S(1)} %get-tuple-element.44), channel_id=1, source_target_pairs={{0,1},{1,0},{2,3},{3,2},{4,5},{5,4},{6,7},{7,6},{8,9},{9,8},{10,11... | collective-permute-start | bytes 3072008 | tf_op jit(solution)/shard_map/ppermute | solution.py:19
  165.0 137.0 %collective-permute-start.12 = (f32[20,160,160]{2,1,0:T(8,128)S(1)}, f32[20,160,160]{2,1,0:T(8,128)S(1)}, u32[]{:S(2)}, u32[]{:S(2)}) collective-permute-start(f32[20,160,160]{2,1,0:T(8,128)S(1)} %collective-permute-done.3.b_ref.refs_7_), channel_id=1, source_target_pairs={{0,2},{2,4},{4,6},{6,8},{8,10},{10,12},{12,14},{14,16},{16,18},{18... | collective-permute-start | bytes 6144008 | tf_op jit(solution)/shard_map/ppermute | solution.py:19
  212.9 102.0 %collective-permute-start.13 = (f32[20,80,160]{2,1,0:T(8,128)}, f32[20,80,160]{2,1,0:T(8,128)S(1)}, u32[]{:S(2)}, u32[]{:S(2)}) collective-permute-start(f32[20,80,160]{2,1,0:T(8,128)} %get-tuple-element.49), channel_id=1, source_target_pairs={{0,1},{1,0},{2,3},{3,2},{4,5},{5,4},{6,7},{7,6},{8,9},{9,8},{10,11... | collective-permute-start | bytes 3072008 | tf_op jit(solution)/shard_map/ppermute | solution.py:19
  232.2 84.0 %collective-permute-start.14 = (f32[20,80,160]{2,1,0:T(8,128)}, f32[20,80,160]{2,1,0:T(8,128)}, u32[]{:S(2)}, u32[]{:S(2)}) collective-permute-start(f32[20,80,160]{2,1,0:T(8,128)} %get-tuple-element.50), channel_id=1, source_target_pairs={{0,1},{1,0},{2,3},{3,2},{4,5},{5,4},{6,7},{7,6},{8,9},{9,8},{10,11... | collective-permute-start | bytes 3072008 | tf_op jit(solution)/shard_map/ppermute | solution.py:19
  268.2 50.8 %collective-permute-start.15 = (f32[20,80,160]{2,1,0:T(8,128)}, f32[20,80,160]{2,1,0:T(8,128)}, u32[]{:S(2)}, u32[]{:S(2)}) collective-permute-start(f32[20,80,160]{2,1,0:T(8,128)} %get-tuple-element.51), channel_id=1, source_target_pairs={{0,1},{1,0},{2,3},{3,2},{4,5},{5,4},{6,7},{7,6},{8,9},{9,8},{10,11... | collective-permute-start | bytes 3072008 | tf_op jit(solution)/shard_map/ppermute | solution.py:19
  309.5 44.5 %collective-permute-start.16 = (f32[20,80,160]{2,1,0:T(8,128)S(1)}, f32[20,80,160]{2,1,0:T(8,128)S(1)}, u32[]{:S(2)}, u32[]{:S(2)}) collective-permute-start(f32[20,80,160]{2,1,0:T(8,128)S(1)} %get-tuple-element.52), channel_id=1, source_target_pairs={{0,1},{1,0},{2,3},{3,2},{4,5},{5,4},{6,7},{7,6},{8,9},{9,8},{10,11... | collective-permute-start | bytes 3072008 | tf_op jit(solution)/shard_map/ppermute | solution.py:19
  405.2 39.5 %collective-permute-start.17 = (f32[20,80,160]{2,1,0:T(8,128)}, f32[20,80,160]{2,1,0:T(8,128)S(1)}, u32[]{:S(2)}, u32[]{:S(2)}) collective-permute-start(f32[20,80,160]{2,1,0:T(8,128)} %copy.29), channel_id=1, source_target_pairs={{0,1},{1,0},{2,3},{3,2},{4,5},{5,4},{6,7},{7,6},{8,9},{9,8},{10,11... | collective-permute-start | bytes 3072008 | tf_op jit(solution)/shard_map/ppermute | solution.py:19
  423.0 52.3 %collective-permute-start.21 = (f32[20,80,160]{2,1,0:T(8,128)}, f32[20,80,160]{2,1,0:T(8,128)}, u32[]{:S(2)}, u32[]{:S(2)}) collective-permute-start(f32[20,80,160]{2,1,0:T(8,128)} %copy.33), channel_id=1, source_target_pairs={{0,1},{1,0},{2,3},{3,2},{4,5},{5,4},{6,7},{7,6},{8,9},{9,8},{10,11... | collective-permute-start | bytes 3072008 | tf_op jit(solution)/shard_map/ppermute | solution.py:19
  425.8 84.6 %collective-permute-start.25 = (f32[20,80,160]{2,1,0:T(8,128)}, f32[20,80,160]{2,1,0:T(8,128)}, u32[]{:S(2)}, u32[]{:S(2)}) collective-permute-start(f32[20,80,160]{2,1,0:T(8,128)} %copy.37), channel_id=1, source_target_pairs={{0,1},{1,0},{2,3},{3,2},{4,5},{5,4},{6,7},{7,6},{8,9},{9,8},{10,11... | collective-permute-start | bytes 3072008 | tf_op jit(solution)/shard_map/ppermute | solution.py:19
  441.1 154.9 %collective-permute-start.8 = (f32[20,80,160]{2,1,0:T(8,128)}, f32[20,80,160]{2,1,0:T(8,128)}, u32[]{:S(2)}, u32[]{:S(2)}) collective-permute-start(f32[20,80,160]{2,1,0:T(8,128)} %copy.27), channel_id=1, source_target_pairs={{0,1},{1,0},{2,3},{3,2},{4,5},{5,4},{6,7},{7,6},{8,9},{9,8},{10,11... | collective-permute-start | bytes 3072008 | tf_op jit(solution)/shard_map/ppermute | solution.py:19
  443.9 136.7 %collective-permute-start.29 = (f32[20,80,160]{2,1,0:T(8,128)}, f32[20,80,160]{2,1,0:T(8,128)}, u32[]{:S(2)}, u32[]{:S(2)}) collective-permute-start(f32[20,80,160]{2,1,0:T(8,128)} %copy.41), channel_id=1, source_target_pairs={{0,1},{1,0},{2,3},{3,2},{4,5},{5,4},{6,7},{7,6},{8,9},{9,8},{10,11... | collective-permute-start | bytes 3072008 | tf_op jit(solution)/shard_map/ppermute | solution.py:19
  452.4 165.0 %collective-permute-start.18 = (f32[20,160,160]{2,1,0:T(8,128)}, f32[20,160,160]{2,1,0:T(8,128)}, u32[]{:S(2)}, u32[]{:S(2)}) collective-permute-start(f32[20,160,160]{2,1,0:T(8,128)} %get-tuple-element.54), channel_id=1, source_target_pairs={{0,30},{2,0},{4,2},{6,4},{8,6},{10,8},{12,10},{14,12},{16,14},{18,... | collective-permute-start | bytes 6144008 | tf_op jit(solution)/shard_map/ppermute | solution.py:19
  483.2 149.7 %collective-permute-start.22 = (f32[20,160,160]{2,1,0:T(8,128)}, f32[20,160,160]{2,1,0:T(8,128)}, u32[]{:S(2)}, u32[]{:S(2)}) collective-permute-start(f32[20,160,160]{2,1,0:T(8,128)} %get-tuple-element.58), channel_id=1, source_target_pairs={{0,30},{2,0},{4,2},{6,4},{8,6},{10,8},{12,10},{14,12},{16,14},{18,... | collective-permute-start | bytes 6144008 | tf_op jit(solution)/shard_map/ppermute | solution.py:19
  510.4 105.2 %collective-permute-start.20 = (f32[20,80,160]{2,1,0:T(8,128)}, f32[20,80,160]{2,1,0:T(8,128)S(1)}, u32[]{:S(2)}, u32[]{:S(2)}) collective-permute-start(f32[20,80,160]{2,1,0:T(8,128)} %copy.31), channel_id=1, source_target_pairs={{0,1},{1,0},{2,3},{3,2},{4,5},{5,4},{6,7},{7,6},{8,9},{9,8},{10,11... | collective-permute-start | bytes 3072008 | tf_op jit(solution)/shard_map/ppermute | solution.py:19
  580.6 77.8 %collective-permute-start.26 = (f32[20,160,160]{2,1,0:T(8,128)}, f32[20,160,160]{2,1,0:T(8,128)}, u32[]{:S(2)}, u32[]{:S(2)}) collective-permute-start(f32[20,160,160]{2,1,0:T(8,128)} %get-tuple-element.62), channel_id=1, source_target_pairs={{0,30},{2,0},{4,2},{6,4},{8,6},{10,8},{12,10},{14,12},{16,14},{18,... | collective-permute-start | bytes 6144008 | tf_op jit(solution)/shard_map/ppermute | solution.py:19
  595.9 89.2 %collective-permute-start.30 = (f32[20,160,160]{2,1,0:T(8,128)}, f32[20,160,160]{2,1,0:T(8,128)}, u32[]{:S(2)}, u32[]{:S(2)}) collective-permute-start(f32[20,160,160]{2,1,0:T(8,128)} %get-tuple-element.66), channel_id=1, source_target_pairs={{0,30},{2,0},{4,2},{6,4},{8,6},{10,8},{12,10},{14,12},{16,14},{18,... | collective-permute-start | bytes 6144008 | tf_op jit(solution)/shard_map/ppermute | solution.py:19
  615.6 34.4 %collective-permute-start.24 = (f32[20,80,160]{2,1,0:T(8,128)}, f32[20,80,160]{2,1,0:T(8,128)}, u32[]{:S(2)}, u32[]{:S(2)}) collective-permute-start(f32[20,80,160]{2,1,0:T(8,128)} %copy.35), channel_id=1, source_target_pairs={{0,1},{1,0},{2,3},{3,2},{4,5},{5,4},{6,7},{7,6},{8,9},{9,8},{10,11... | collective-permute-start | bytes 3072008 | tf_op jit(solution)/shard_map/ppermute | solution.py:19
  617.4 67.7 %collective-permute-start.28 = (f32[20,80,160]{2,1,0:T(8,128)}, f32[20,80,160]{2,1,0:T(8,128)}, u32[]{:S(2)}, u32[]{:S(2)}) collective-permute-start(f32[20,80,160]{2,1,0:T(8,128)} %copy.39), channel_id=1, source_target_pairs={{0,1},{1,0},{2,3},{3,2},{4,5},{5,4},{6,7},{7,6},{8,9},{9,8},{10,11... | collective-permute-start | bytes 3072008 | tf_op jit(solution)/shard_map/ppermute | solution.py:19
  633.0 64.5 %collective-permute-start.19 = (f32[20,160,160]{2,1,0:T(8,128)}, f32[20,160,160]{2,1,0:T(8,128)S(1)}, u32[]{:S(2)}, u32[]{:S(2)}) collective-permute-start(f32[20,160,160]{2,1,0:T(8,128)} %get-tuple-element.56), channel_id=1, source_target_pairs={{0,30},{2,0},{4,2},{6,4},{8,6},{10,8},{12,10},{14,12},{16,14},{18,... | collective-permute-start | bytes 6144008 | tf_op jit(solution)/shard_map/ppermute | solution.py:19
  650.0 81.2 %collective-permute-start.23 = (f32[20,160,160]{2,1,0:T(8,128)}, f32[20,160,160]{2,1,0:T(8,128)S(1)}, u32[]{:S(2)}, u32[]{:S(2)}) collective-permute-start(f32[20,160,160]{2,1,0:T(8,128)} %get-tuple-element.60), channel_id=1, source_target_pairs={{0,30},{2,0},{4,2},{6,4},{8,6},{10,8},{12,10},{14,12},{16,14},{18,... | collective-permute-start | bytes 6144008 | tf_op jit(solution)/shard_map/ppermute | solution.py:19
  669.7 96.8 %collective-permute-start.27 = (f32[20,160,160]{2,1,0:T(8,128)}, f32[20,160,160]{2,1,0:T(8,128)}, u32[]{:S(2)}, u32[]{:S(2)}) collective-permute-start(f32[20,160,160]{2,1,0:T(8,128)} %get-tuple-element.64), channel_id=1, source_target_pairs={{0,30},{2,0},{4,2},{6,4},{8,6},{10,8},{12,10},{14,12},{16,14},{18,... | collective-permute-start | bytes 6144008 | tf_op jit(solution)/shard_map/ppermute | solution.py:19
  693.0 108.4 %collective-permute-start.31 = (f32[20,160,160]{2,1,0:T(8,128)S(1)}, f32[20,160,160]{2,1,0:T(8,128)S(1)}, u32[]{:S(2)}, u32[]{:S(2)}) collective-permute-start(f32[20,160,160]{2,1,0:T(8,128)S(1)} %get-tuple-element.68), channel_id=1, source_target_pairs={{0,30},{2,0},{4,2},{6,4},{8,6},{10,8},{12,10},{14,12},{16,14},{18,... | collective-permute-start | bytes 6144008 | tf_op jit(solution)/shard_map/ppermute | solution.py:19
  (44 other events, 723.1 us)

commit v2 on v1

--- a/solution.py
+++ b/solution.py
@@ -181,19 +181,27 @@
         field = field * kernel
         return jnp.einsum("kz,kyx->zyx", table_z, field, precision=high)
 
+    arrived = []
+
     def gathered(field, start):
         parts = []
         for j in range(groups):
             part = field[j * local + start : j * local + start + depth]
-            parts.append(passed_along(part, "slab", -j) if j else part)
+            if j:
+                if len(arrived) >= 2 * (groups - 1):
+                    part, _ = lax.optimization_barrier((part, arrived[-2 * (groups - 1)]))
+                part = passed_along(part, "slab", -j)
+                arrived.append(part)
+            parts.append(part)
         return parts
 
     near = [passed_along(resident[s : s + depth], "band", 1) for s in starts]
     far = [passed_along(part, "band", 1) for part in near]
     near_parts = spread(near)
     far_parts = spread(far)
+    near_field = filtered(near_parts)
+    far_parts[-1], near_field = lax.optimization_barrier((far_parts[-1], near_field))
     far_field = filtered(far_parts)
-    near_field = filtered(near_parts)
     carried = []
     for chunk, start in enumerate(starts):
         parts = gathered(far_field, start)

time: 817 us -> 834 us (1.021)
  starting transfers between devices: 61.4 us -> 81 us
  local copies, waits for them, and re-layouts: 90.1 us -> 103 us
  matrix products: 86.6 us -> 74.6 us
    optimization_barrier x0 -> x3, local copies, waits for them, and re-layouts: none -> 21.9 us  [the longest x1 17 us: shards(): lax.optimization_barrier((far_parts[-1], near_field))]
    ppermute x32, starting transfers between devices: 61.4 us -> 81 us  [passed_along(): return lax.ppermute(value, axis, pairs)]
    dot_general x2, matrix products: 55.4 us -> 45.6 us  [filtered(): field = jnp.einsum('kz,zyx->kyx', table_z, field, precision=high)]
    unnamed x118 -> x112, local copies, waits for them, and re-layouts: 57.1 us -> 54.4 us
  transfers between devices with their start and end apart: 32 -> 32, of which waited for: 18 -> 21; matrix products, arithmetic and copies ran while one was open for 13% -> 13% of each run, Pallas kernels for 16% -> 15%
where the time goes in v2:
time: 834 us; the launch traced here: 827 us
  waiting for transfers between devices  425 us (51%)
  Pallas kernels  128 us (15%)
  local copies, waits for them, and re-layouts  103 us (12%)
  starting transfers between devices  81 us (10%)
  matrix products  74.6 us (9%)
  other arithmetic  14.4 us (2%)
    ppermute x32, waiting for transfers between devices, passed_along(): return lax.ppermute(value, axis, pairs)  425 us
    ppermute x32, starting transfers between devices, passed_along(): return lax.ppermute(value, axis, pairs)  81 us
    pallas_call x8, Pallas kernels, inverse(): pl.pallas_call(functools.partial(inverse_kernel, groups, bool(extra)), gr...  68.2 us
    pallas_call x8, Pallas kernels, forward(): pl.pallas_call(forward_kernel, grid=(depth // block,), in_specs=[pl.Block...  59.6 us
    unnamed x112, local copies, waits for them, and re-layouts  54.4 us
    dot_general x2, matrix products, filtered(): field = jnp.einsum('kz,zyx->kyx', table_z, field, precision=high)  45.6 us
    dot_general x2, matrix products, filtered(): return jnp.einsum('kz,kyx->zyx', table_z, field, precision=high)  28.9 us
    optimization_barrier x1, local copies, waits for them, and re-layouts, shards(): lax.optimization_barrier((far_parts[-1], near_field))  17 us
  transfers between devices with their start and end apart: 32, of which 21 were waited for; matrix products, arithmetic and copies ran while one was open for 13% of the time, Pallas kernels for 15%

profile of v2, /device:TPU:1, one launch (start us, length us, event | category | flops | bytes accessed | tf_op | source)
XLA Modules:
  0.0 826.8 jit_solution(3095458475765921331)
XLA Ops:
  0.0 10.0 %slice_bitcast_fusion = (f32[20,160,160]{2,1,0:T(8,128)}, f32[20,160,160]{2,1,0:T(8,128)}, f32[20,160,160]{2,1,0:T(8,128)}, f32[20,160,160]{2,1,0:T(8,128)}) fusion(f32[1,80,160,160]{3,2,1,0:T(8,128)} %param.1), kind=kLoop, calls=%fused_computation.14 | loop fusion | bytes 16384000 | tf_op jit(solution)/shard_map/slice | solution.py:198
  17.2 31.4 %collective-permute-done.3.b_ref.refs_7_ = f32[20,160,160]{2,1,0:T(8,128)} collective-permute-done((f32[20,160,160]{2,1,0:T(8,128)}, f32[20,160,160]{2,1,0:T(8,128)}, u32[]{:S(2)}, u32[]{:S(2)}) %collective-permute-start.3) | collective-permute-done | bytes 2048032 | tf_op jit(solution)/shard_map/ppermute | solution.py:19
  58.8 24.9 %collective-permute-done.4.b_ref.refs_7_ = f32[20,160,160]{2,1,0:T(8,128)} collective-permute-done((f32[20,160,160]{2,1,0:T(8,128)}, f32[20,160,160]{2,1,0:T(8,128)}, u32[]{:S(2)}, u32[]{:S(2)}) %collective-permute-start.4) | collective-permute-done | bytes 2048032 | tf_op jit(solution)/shard_map/ppermute | solution.py:19
  93.9 24.9 %collective-permute-done.5.b_ref.refs_7_ = f32[20,160,160]{2,1,0:T(8,128)} collective-permute-done((f32[20,160,160]{2,1,0:T(8,128)}, f32[20,160,160]{2,1,0:T(8,128)}, u32[]{:S(2)}, u32[]{:S(2)}) %collective-permute-start.5) | collective-permute-done | bytes 2048032 | tf_op jit(solution)/shard_map/ppermute | solution.py:19
  130.1 23.8 %collective-permute-done.b_ref.refs_7_ = f32[20,160,160]{2,1,0:T(8,128)S(1)} collective-permute-done((f32[20,160,160]{2,1,0:T(8,128)}, f32[20,160,160]{2,1,0:T(8,128)S(1)}, u32[]{:S(2)}, u32[]{:S(2)}) %collective-permute-start) | collective-permute-done | bytes 2048032 | tf_op jit(solution)/shard_map/ppermute | solution.py:19
  180.8 17.7 %collective-permute-done.9 = f32[20,80,160]{2,1,0:T(8,128)S(1)} collective-permute-done((f32[20,80,160]{2,1,0:T(8,128)S(1)}, f32[20,80,160]{2,1,0:T(8,128)S(1)}, u32[]{:S(2)}, u32[]{:S(2)}) %collective-permute-start.9) | collective-permute-done | bytes 1024032 | tf_op jit(solution)/shard_map/ppermute | solution.py:19
  199.7 22.8 %fusion.5 = f32[160,80,160]{2,0,1:T(8,128)} fusion(f32[160,80,160]{2,1,0:T(8,128)} %constant_dynamic-update-slice_fusion, s32[160]{0:T(256)S(1)} %pad_add_fusion), kind=kOutput, calls=%fused_computation.8 | convolution fusion | flops 1966336000 | bytes 16384640 | tf_op jit(solution)/shard_map/kz,zyx->kyx/dot_general | solution.py:180
  243.8 26.8 %collective-permute-done.12.b_ref.refs_7_ = f32[20,160,160]{2,1,0:T(8,128)S(1)} collective-permute-done((f32[20,160,160]{2,1,0:T(8,128)}, f32[20,160,160]{2,1,0:T(8,128)S(1)}, u32[]{:S(2)}, u32[]{:S(2)}) %collective-permute-start.12) | collective-permute-done | bytes 2048032 | tf_op jit(solution)/shard_map/ppermute | solution.py:19
  278.2 27.4 %collective-permute-done.1.b_ref.refs_7_ = f32[20,160,160]{2,1,0:T(8,128)S(1)} collective-permute-done((f32[20,160,160]{2,1,0:T(8,128)S(1)}, f32[20,160,160]{2,1,0:T(8,128)S(1)}, u32[]{:S(2)}, u32[]{:S(2)}) %collective-permute-start.1) | collective-permute-done | bytes 2048032 | tf_op jit(solution)/shard_map/ppermute | solution.py:19
  313.2 15.9 %fusion.9 = f32[160,80,160]{2,0,1:T(8,128)} fusion(f32[160,80,160]{2,0,1:T(8,128)} %fusion.5, f32[160]{0:T(256)S(1)} %multiply_multiply_fusion, f32[160,80]{0,1:T(8,128)S(1)} %broadcast_add_fusion, s32[160]{0:T(256)S(1)} %pad_add_fusion), kind=kOutput, calls=%fused_computation.12 | convolution fusion | flops 1980672000 | bytes 16436480 | tf_op jit(solution)/shard_map/kz,kyx->zyx/dot_general | solution.py:182
  334.3 35.6 %collective-permute-done.2 = f32[20,80,160]{2,1,0:T(8,128)S(1)} collective-permute-done((f32[20,80,160]{2,1,0:T(8,128)S(1)}, f32[20,80,160]{2,1,0:T(8,128)S(1)}, u32[]{:S(2)}, u32[]{:S(2)}) %collective-permute-start.2) | collective-permute-done | bytes 1024032 | tf_op jit(solution)/shard_map/ppermute | solution.py:19
  378.1 22.8 %fusion.3 = f32[160,80,160]{2,0,1:T(8,128)} fusion(f32[160,80,160]{2,1,0:T(8,128)} %constant_dynamic-update-slice_fusion.8, s32[160]{0:T(256)S(1)} %pad_add_fusion), kind=kOutput, calls=%fused_computation.6 | convolution fusion | flops 1966336000 | bytes 16384640 | tf_op jit(solution)/shard_map/kz,zyx->kyx/dot_general | solution.py:180
  400.9 13.0 %fusion.7 = f32[160,80,160]{2,0,1:T(8,128)S(1)} fusion(f32[160,80,160]{2,0,1:T(8,128)} %fusion.3, f32[160]{0:T(256)S(1)} %multiply_multiply_fusion, f32[160,80]{0,1:T(8,128)S(1)} %broadcast_add_fusion, s32[160]{0:T(256)S(1)} %pad_add_fusion), kind=kOutput, calls=%fused_computation.10 | convolution fusion | flops 1980672000 | bytes 16436480 | tf_op jit(solution)/shard_map/kz,kyx->zyx/dot_general | solution.py:182
  425.8 28.0 %collective-permute-done.16.refs_1_ = f32[20,80,160]{2,1,0:T(8,128)S(1)} collective-permute-done((f32[20,80,160]{2,1,0:T(8,128)S(1)}, f32[20,80,160]{2,1,0:T(8,128)S(1)}, u32[]{:S(2)}, u32[]{:S(2)}) %collective-permute-start.16) | collective-permute-done | bytes 1024032 | tf_op jit(solution)/shard_map/ppermute | solution.py:19
  456.4 17.0 %copy.3 = f32[160,80,160]{2,1,0:T(8,128)} copy(f32[160,80,160]{2,0,1:T(8,128)} %fusion.9) | data formatting | bytes 16384000 | tf_op jit(solution)/shard_map/optimization_barrier | solution.py:203
  476.6 12.4 %collective-permute-done.21.refs_1_ = f32[20,80,160]{2,1,0:T(8,128)} collective-permute-done((f32[20,80,160]{2,1,0:T(8,128)}, f32[20,80,160]{2,1,0:T(8,128)}, u32[]{:S(2)}, u32[]{:S(2)}) %collective-permute-start.21) | collective-permute-done | bytes 1024032 | tf_op jit(solution)/shard_map/ppermute | solution.py:19
  490.3 9.7 %fusion.59 = (f32[20,80,160]{2,1,0:T(8,128)}, f32[20,80,160]{2,1,0:T(8,128)}, f32[20,80,160]{2,1,0:T(8,128)}, f32[20,80,160]{2,1,0:T(8,128)}, f32[20,80,160]{2,1...) fusion(f32[160,80,160]{2,1,0:T(8,128)} %copy.3), kind=kLoop, calls=%fused_computation.105 | loop fusion | bytes 16384000 | tf_op jit(solution)/shard_map/slice | solution.py:189
  511.7 12.5 %collective-permute-done.17.refs_1_ = f32[20,80,160]{2,1,0:T(8,128)} collective-permute-done((f32[20,80,160]{2,1,0:T(8,128)}, f32[20,80,160]{2,1,0:T(8,128)}, u32[]{:S(2)}, u32[]{:S(2)}) %collective-permute-start.17) | collective-permute-done | bytes 1024032 | tf_op jit(solution)/shard_map/ppermute | solution.py:19
  525.4 10.5 %collective-permute-start.19 = (f32[20,160,160]{2,1,0:T(8,128)}, f32[20,160,160]{2,1,0:T(8,128)}, u32[]{:S(2)}, u32[]{:S(2)}) collective-permute-start(f32[20,160,160]{2,1,0:T(8,128)} %get-tuple-element.66), channel_id=1, source_target_pairs={{0,30},{2,0},{4,2},{6,4},{8,6},{10,8},{12,10},{14,12},{16,14},{18,... | collective-permute-start | bytes 6144008 | tf_op jit(solution)/shard_map/ppermute | solution.py:19
  537.9 8.0 inverse.10
  547.7 11.6 %collective-permute-done.22.refs_1_ = f32[20,80,160]{2,1,0:T(8,128)} collective-permute-done((f32[20,80,160]{2,1,0:T(8,128)}, f32[20,80,160]{2,1,0:T(8,128)}, u32[]{:S(2)}, u32[]{:S(2)}) %collective-permute-start.22) | collective-permute-done | bytes 1024032 | tf_op jit(solution)/shard_map/ppermute | solution.py:19
  569.0 10.3 %collective-permute-start.27 = (f32[20,160,160]{2,1,0:T(8,128)}, f32[20,160,160]{2,1,0:T(8,128)}, u32[]{:S(2)}, u32[]{:S(2)}) collective-permute-start(f32[20,160,160]{2,1,0:T(8,128)} %get-tuple-element.77), channel_id=1, source_target_pairs={{0,30},{2,0},{4,2},{6,4},{8,6},{10,8},{12,10},{14,12},{16,14},{18,... | collective-permute-start | bytes 6144008 | tf_op jit(solution)/shard_map/ppermute | solution.py:19
  595.5 10.3 %collective-permute-start.30 = (f32[20,160,160]{2,1,0:T(8,128)}, f32[20,160,160]{2,1,0:T(8,128)S(1)}, u32[]{:S(2)}, u32[]{:S(2)}) collective-permute-start(f32[20,160,160]{2,1,0:T(8,128)} %get-tuple-element.82), channel_id=1, source_target_pairs={{0,30},{2,0},{4,2},{6,4},{8,6},{10,8},{12,10},{14,12},{16,14},{18,... | collective-permute-start | bytes 6144008 | tf_op jit(solution)/shard_map/ppermute | solution.py:19
  605.7 23.7 %collective-permute-done.23.refs_1_ = f32[20,80,160]{2,1,0:T(8,128)S(1)} collective-permute-done((f32[20,80,160]{2,1,0:T(8,128)}, f32[20,80,160]{2,1,0:T(8,128)S(1)}, u32[]{:S(2)}, u32[]{:S(2)}) %collective-permute-start.23) | collective-permute-done | bytes 1024032 | tf_op jit(solution)/shard_map/ppermute | solution.py:19
  633.5 9.5 %inverse.9 = (f32[20,160,160]{2,1,0:T(8,128)S(1)}, f32[20,160,160]{2,1,0:T(8,128)}) custom-call(f32[20,80,160]{2,1,0:T(8,128)S(1)} %copy-done.18, f32[20,80,160]{2,1,0:T(8,128)S(1)} %copy-done.28, bf16[160,160]{1,0:T(8,128)(2,1)S(1)} %get-tuple-element.109.xu_ref.refs_2_, bf16[160,160]{1,0:T(8,128)(2,1)S(1)} %get-tuple-element.110.xl_ref.refs_3_, ...), custom_call_target="tpu_custom_call" | custom-call | flops 983040000 | bytes 14336000 | tf_op jit(solution)/shard_map/inverse/pallas_call | solution.py:131
  649.6 9.4 %inverse.11 = (f32[20,160,160]{2,1,0:T(8,128)S(1)}, f32[20,160,160]{2,1,0:T(8,128)}) custom-call(f32[20,80,160]{2,1,0:T(8,128)S(1)} %copy-done.17, f32[20,80,160]{2,1,0:T(8,128)S(1)} %copy-done.30, bf16[160,160]{1,0:T(8,128)(2,1)S(1)} %get-tuple-element.109.xu_ref.refs_2_, bf16[160,160]{1,0:T(8,128)(2,1)S(1)} %get-tuple-element.110.xl_ref.refs_3_, ...), custom_call_target="tpu_custom_call" | custom-call | flops 983040000 | bytes 14336000 | tf_op jit(solution)/shard_map/inverse/pallas_call | solution.py:131
  663.8 9.7 %inverse.13 = (f32[20,160,160]{2,1,0:T(8,128)S(1)}, f32[20,160,160]{2,1,0:T(8,128)}) custom-call(f32[20,80,160]{2,1,0:T(8,128)S(1)} %copy-done.16, f32[20,80,160]{2,1,0:T(8,128)} %collective-permute-done.26.refs_1_, bf16[160,160]{1,0:T(8,128)(2,1)S(1)} %get-tuple-element.109.xu_ref.refs_2_, bf16[160,160]{1,0:T(8,128)(2,1)S(1)} %get-tuple-element.110.xl_ref.refs_3_, ...), custom_call_target="tpu_custom_call" | custom-call | flops 983040000 | bytes 14336000 | tf_op jit(solution)/shard_map/inverse/pallas_call | solution.py:131
  675.1 12.0 %collective-permute-start.28 = (f32[20,160,160]{2,1,0:T(8,128)}, f32[20,160,160]{2,1,0:T(8,128)S(1)}, u32[]{:S(2)}, u32[]{:S(2)}) collective-permute-start(f32[20,160,160]{2,1,0:T(8,128)} %get-tuple-element.79), channel_id=1, source_target_pairs={{0,30},{2,0},{4,2},{6,4},{8,6},{10,8},{12,10},{14,12},{16,14},{18,... | collective-permute-start | bytes 6144008 | tf_op jit(solution)/shard_map/ppermute | solution.py:19
  687.1 11.8 %collective-permute-done.29.refs_1_ = f32[20,80,160]{2,1,0:T(8,128)} collective-permute-done((f32[20,80,160]{2,1,0:T(8,128)}, f32[20,80,160]{2,1,0:T(8,128)}, u32[]{:S(2)}, u32[]{:S(2)}) %collective-permute-start.29) | collective-permute-done | bytes 1024032 | tf_op jit(solution)/shard_map/ppermute | solution.py:19
  717.9 32.6 %collective-permute-done.25 = f32[20,160,160]{2,1,0:T(8,128)} collective-permute-done((f32[20,160,160]{2,1,0:T(8,128)}, f32[20,160,160]{2,1,0:T(8,128)}, u32[]{:S(2)}, u32[]{:S(2)}) %collective-permute-start.25) | collective-permute-done | bytes 2048032 | tf_op jit(solution)/shard_map/ppermute | solution.py:19
  753.1 32.4 %collective-permute-done.28 = f32[20,160,160]{2,1,0:T(8,128)S(1)} collective-permute-done((f32[20,160,160]{2,1,0:T(8,128)}, f32[20,160,160]{2,1,0:T(8,128)S(1)}, u32[]{:S(2)}, u32[]{:S(2)}) %collective-permute-start.28) | collective-permute-done | bytes 2048032 | tf_op jit(solution)/shard_map/ppermute | solution.py:19
  786.0 34.6 %collective-permute-done.31 = f32[20,160,160]{2,1,0:T(8,128)S(1)} collective-permute-done((f32[20,160,160]{2,1,0:T(8,128)S(1)}, f32[20,160,160]{2,1,0:T(8,128)S(1)}, u32[]{:S(2)}, u32[]{:S(2)}) %collective-permute-start.31) | collective-permute-done | bytes 2048032 | tf_op jit(solution)/shard_map/ppermute | solution.py:19
  (185 shorter events, 223.0 us)
Async XLA Ops:
  10.0 38.6 %collective-permute-start.3 = (f32[20,160,160]{2,1,0:T(8,128)}, f32[20,160,160]{2,1,0:T(8,128)}, u32[]{:S(2)}, u32[]{:S(2)}) collective-permute-start(f32[20,160,160]{2,1,0:T(8,128)} %get-tuple-element.102), channel_id=1, source_target_pairs={{0,2},{2,4},{4,6},{6,8},{8,10},{10,12},{12,14},{14,16},{16,18},{18... | collective-permute-start | bytes 6144008 | tf_op jit(solution)/shard_map/ppermute | solution.py:19
  12.6 71.0 %collective-permute-start.4 = (f32[20,160,160]{2,1,0:T(8,128)}, f32[20,160,160]{2,1,0:T(8,128)}, u32[]{:S(2)}, u32[]{:S(2)}) collective-permute-start(f32[20,160,160]{2,1,0:T(8,128)} %get-tuple-element.104), channel_id=1, source_target_pairs={{0,2},{2,4},{4,6},{6,8},{8,10},{10,12},{12,14},{14,16},{16,18},{18... | collective-permute-start | bytes 6144008 | tf_op jit(solution)/shard_map/ppermute | solution.py:19
  12.7 106.1 %collective-permute-start.5 = (f32[20,160,160]{2,1,0:T(8,128)}, f32[20,160,160]{2,1,0:T(8,128)}, u32[]{:S(2)}, u32[]{:S(2)}) collective-permute-start(f32[20,160,160]{2,1,0:T(8,128)} %get-tuple-element.101), channel_id=1, source_target_pairs={{0,2},{2,4},{4,6},{6,8},{8,10},{10,12},{12,14},{14,16},{16,18},{18... | collective-permute-start | bytes 6144008 | tf_op jit(solution)/shard_map/ppermute | solution.py:19
  14.3 139.6 %collective-permute-start = (f32[20,160,160]{2,1,0:T(8,128)}, f32[20,160,160]{2,1,0:T(8,128)S(1)}, u32[]{:S(2)}, u32[]{:S(2)}) collective-permute-start(f32[20,160,160]{2,1,0:T(8,128)} %get-tuple-element.103), channel_id=1, source_target_pairs={{0,2},{2,4},{4,6},{6,8},{8,10},{10,12},{12,14},{14,16},{16,18},{18... | collective-permute-start | bytes 6144008 | tf_op jit(solution)/shard_map/ppermute | solution.py:19
  57.6 108.1 %collective-permute-start.6 = (f32[20,80,160]{2,1,0:T(8,128)}, f32[20,80,160]{2,1,0:T(8,128)}, u32[]{:S(2)}, u32[]{:S(2)}) collective-permute-start(f32[20,80,160]{2,1,0:T(8,128)} %get-tuple-element.50), channel_id=1, source_target_pairs={{0,1},{1,0},{2,3},{3,2},{4,5},{5,4},{6,7},{7,6},{8,9},{9,8},{10,11... | collective-permute-start | bytes 3072008 | tf_op jit(solution)/shard_map/ppermute | solution.py:19
  92.7 73.1 %collective-permute-start.7 = (f32[20,80,160]{2,1,0:T(8,128)}, f32[20,80,160]{2,1,0:T(8,128)}, u32[]{:S(2)}, u32[]{:S(2)}) collective-permute-start(f32[20,80,160]{2,1,0:T(8,128)} %get-tuple-element.51), channel_id=1, source_target_pairs={{0,1},{1,0},{2,3},{3,2},{4,5},{5,4},{6,7},{7,6},{8,9},{9,8},{10,11... | collective-permute-start | bytes 3072008 | tf_op jit(solution)/shard_map/ppermute | solution.py:19
  128.6 40.9 %collective-permute-start.8 = (f32[20,80,160]{2,1,0:T(8,128)S(1)}, f32[20,80,160]{2,1,0:T(8,128)}, u32[]{:S(2)}, u32[]{:S(2)}) collective-permute-start(f32[20,80,160]{2,1,0:T(8,128)S(1)} %get-tuple-element.52), channel_id=1, source_target_pairs={{0,1},{1,0},{2,3},{3,2},{4,5},{5,4},{6,7},{7,6},{8,9},{9,8},{10,11... | collective-permute-start | bytes 3072008 | tf_op jit(solution)/shard_map/ppermute | solution.py:19
  160.5 37.9 %collective-permute-start.9 = (f32[20,80,160]{2,1,0:T(8,128)S(1)}, f32[20,80,160]{2,1,0:T(8,128)S(1)}, u32[]{:S(2)}, u32[]{:S(2)}) collective-permute-start(f32[20,80,160]{2,1,0:T(8,128)S(1)} %get-tuple-element.53), channel_id=1, source_target_pairs={{0,1},{1,0},{2,3},{3,2},{4,5},{5,4},{6,7},{7,6},{8,9},{9,8},{10,11... | collective-permute-start | bytes 3072008 | tf_op jit(solution)/shard_map/ppermute | solution.py:19
  161.8 60.8 %collective-permute-start.10 = (f32[20,160,160]{2,1,0:T(8,128)}, f32[20,160,160]{2,1,0:T(8,128)S(1)}, u32[]{:S(2)}, u32[]{:S(2)}) collective-permute-start(f32[20,160,160]{2,1,0:T(8,128)} %collective-permute-done.3.b_ref.refs_7_), channel_id=1, source_target_pairs={{0,2},{2,4},{4,6},{6,8},{8,10},{10,12},{12,14},{14,16},{16,18},{18... | collective-permute-start | bytes 6144008 | tf_op jit(solution)/shard_map/ppermute | solution.py:19
  165.7 69.8 %collective-permute-start.11 = (f32[20,160,160]{2,1,0:T(8,128)}, f32[20,160,160]{2,1,0:T(8,128)S(1)}, u32[]{:S(2)}, u32[]{:S(2)}) collective-permute-start(f32[20,160,160]{2,1,0:T(8,128)} %collective-permute-done.4.b_ref.refs_7_), channel_id=1, source_target_pairs={{0,2},{2,4},{4,6},{6,8},{8,10},{10,12},{12,14},{14,16},{16,18},{18... | collective-permute-start | bytes 6144008 | tf_op jit(solution)/shard_map/ppermute | solution.py:19
  165.7 104.9 %collective-permute-start.12 = (f32[20,160,160]{2,1,0:T(8,128)}, f32[20,160,160]{2,1,0:T(8,128)S(1)}, u32[]{:S(2)}, u32[]{:S(2)}) collective-permute-start(f32[20,160,160]{2,1,0:T(8,128)} %collective-permute-done.5.b_ref.refs_7_), channel_id=1, source_target_pairs={{0,2},{2,4},{4,6},{6,8},{8,10},{10,12},{12,14},{14,16},{16,18},{18... | collective-permute-start | bytes 6144008 | tf_op jit(solution)/shard_map/ppermute | solution.py:19
  169.6 136.0 %collective-permute-start.1 = (f32[20,160,160]{2,1,0:T(8,128)S(1)}, f32[20,160,160]{2,1,0:T(8,128)S(1)}, u32[]{:S(2)}, u32[]{:S(2)}) collective-permute-start(f32[20,160,160]{2,1,0:T(8,128)S(1)} %collective-permute-done.b_ref.refs_7_), channel_id=1, source_target_pairs={{0,2},{2,4},{4,6},{6,8},{8,10},{10,12},{12,14},{14,16},{16,18},{18... | collective-permute-start | bytes 6144008 | tf_op jit(solution)/shard_map/ppermute | solution.py:19
  230.6 139.3 %collective-permute-start.13 = (f32[20,80,160]{2,1,0:T(8,128)}, f32[20,80,160]{2,1,0:T(8,128)}, u32[]{:S(2)}, u32[]{:S(2)}) collective-permute-start(f32[20,80,160]{2,1,0:T(8,128)} %get-tuple-element.59), channel_id=1, source_target_pairs={{0,1},{1,0},{2,3},{3,2},{4,5},{5,4},{6,7},{7,6},{8,9},{9,8},{10,11... | collective-permute-start | bytes 3072008 | tf_op jit(solution)/shard_map/ppermute | solution.py:19
  243.5 129.2 %collective-permute-start.14 = (f32[20,80,160]{2,1,0:T(8,128)}, f32[20,80,160]{2,1,0:T(8,128)S(1)}, u32[]{:S(2)}, u32[]{:S(2)}) collective-permute-start(f32[20,80,160]{2,1,0:T(8,128)} %get-tuple-element.60), channel_id=1, source_target_pairs={{0,1},{1,0},{2,3},{3,2},{4,5},{5,4},{6,7},{7,6},{8,9},{9,8},{10,11... | collective-permute-start | bytes 3072008 | tf_op jit(solution)/shard_map/ppermute | solution.py:19
  277.8 96.2 %collective-permute-start.15 = (f32[20,80,160]{2,1,0:T(8,128)S(1)}, f32[20,80,160]{2,1,0:T(8,128)}, u32[]{:S(2)}, u32[]{:S(2)}) collective-permute-start(f32[20,80,160]{2,1,0:T(8,128)S(1)} %get-tuple-element.61), channel_id=1, source_target_pairs={{0,1},{1,0},{2,3},{3,2},{4,5},{5,4},{6,7},{7,6},{8,9},{9,8},{10,11... | collective-permute-start | bytes 3072008 | tf_op jit(solution)/shard_map/ppermute | solution.py:19
  312.9 57.1 %collective-permute-start.2 = (f32[20,80,160]{2,1,0:T(8,128)S(1)}, f32[20,80,160]{2,1,0:T(8,128)S(1)}, u32[]{:S(2)}, u32[]{:S(2)}) collective-permute-start(f32[20,80,160]{2,1,0:T(8,128)S(1)} %get-tuple-element.45), channel_id=1, source_target_pairs={{0,1},{1,0},{2,3},{3,2},{4,5},{5,4},{6,7},{7,6},{8,9},{9,8},{10,11... | collective-permute-start | bytes 3072008 | tf_op jit(solution)/shard_map/ppermute | solution.py:19
  420.9 32.9 %collective-permute-start.16 = (f32[20,80,160]{2,1,0:T(8,128)S(1)}, f32[20,80,160]{2,1,0:T(8,128)S(1)}, u32[]{:S(2)}, u32[]{:S(2)}) collective-permute-start(f32[20,80,160]{2,1,0:T(8,128)S(1)} %copy.27), channel_id=1, source_target_pairs={{0,1},{1,0},{2,3},{3,2},{4,5},{5,4},{6,7},{7,6},{8,9},{9,8},{10,11... | collective-permute-start | bytes 3072008 | tf_op jit(solution)/shard_map/ppermute | solution.py:19
  423.9 65.1 %collective-permute-start.21 = (f32[20,80,160]{2,1,0:T(8,128)}, f32[20,80,160]{2,1,0:T(8,128)}, u32[]{:S(2)}, u32[]{:S(2)}) collective-permute-start(f32[20,80,160]{2,1,0:T(8,128)} %copy.30), channel_id=1, source_target_pairs={{0,1},{1,0},{2,3},{3,2},{4,5},{5,4},{6,7},{7,6},{8,9},{9,8},{10,11... | collective-permute-start | bytes 3072008 | tf_op jit(solution)/shard_map/ppermute | solution.py:19
  455.1 69.1 %collective-permute-start.17 = (f32[20,80,160]{2,1,0:T(8,128)}, f32[20,80,160]{2,1,0:T(8,128)}, u32[]{:S(2)}, u32[]{:S(2)}) collective-permute-start(f32[20,80,160]{2,1,0:T(8,128)} %copy.26), channel_id=1, source_target_pairs={{0,1},{1,0},{2,3},{3,2},{4,5},{5,4},{6,7},{7,6},{8,9},{9,8},{10,11... | collective-permute-start | bytes 3072008 | tf_op jit(solution)/shard_map/ppermute | solution.py:19
  489.1 70.2 %collective-permute-start.22 = (f32[20,80,160]{2,1,0:T(8,128)}, f32[20,80,160]{2,1,0:T(8,128)}, u32[]{:S(2)}, u32[]{:S(2)}) collective-permute-start(f32[20,80,160]{2,1,0:T(8,128)} %copy.29), channel_id=1, source_target_pairs={{0,1},{1,0},{2,3},{3,2},{4,5},{5,4},{6,7},{7,6},{8,9},{9,8},{10,11... | collective-permute-start | bytes 3072008 | tf_op jit(solution)/shard_map/ppermute | solution.py:19
  524.2 70.1 %collective-permute-start.18 = (f32[20,80,160]{2,1,0:T(8,128)S(1)}, f32[20,80,160]{2,1,0:T(8,128)S(1)}, u32[]{:S(2)}, u32[]{:S(2)}) collective-permute-start(f32[20,80,160]{2,1,0:T(8,128)S(1)} %copy-done.45), channel_id=1, source_target_pairs={{0,1},{1,0},{2,3},{3,2},{4,5},{5,4},{6,7},{7,6},{8,9},{9,8},{10,11... | collective-permute-start | bytes 3072008 | tf_op jit(solution)/shard_map/ppermute | solution.py:19
  525.4 106.4 %collective-permute-start.19 = (f32[20,160,160]{2,1,0:T(8,128)}, f32[20,160,160]{2,1,0:T(8,128)}, u32[]{:S(2)}, u32[]{:S(2)}) collective-permute-start(f32[20,160,160]{2,1,0:T(8,128)} %get-tuple-element.66), channel_id=1, source_target_pairs={{0,30},{2,0},{4,2},{6,4},{8,6},{10,8},{12,10},{14,12},{16,14},{18,... | collective-permute-start | bytes 6144008 | tf_op jit(solution)/shard_map/ppermute | solution.py:19
  547.7 95.3 %collective-permute-start.24 = (f32[20,160,160]{2,1,0:T(8,128)}, f32[20,160,160]{2,1,0:T(8,128)}, u32[]{:S(2)}, u32[]{:S(2)}) collective-permute-start(f32[20,160,160]{2,1,0:T(8,128)} %get-tuple-element.72), channel_id=1, source_target_pairs={{0,30},{2,0},{4,2},{6,4},{8,6},{10,8},{12,10},{14,12},{16,14},{18,... | collective-permute-start | bytes 6144008 | tf_op jit(solution)/shard_map/ppermute | solution.py:19
  569.0 91.8 %collective-permute-start.27 = (f32[20,160,160]{2,1,0:T(8,128)}, f32[20,160,160]{2,1,0:T(8,128)}, u32[]{:S(2)}, u32[]{:S(2)}) collective-permute-start(f32[20,160,160]{2,1,0:T(8,128)} %get-tuple-element.77), channel_id=1, source_target_pairs={{0,30},{2,0},{4,2},{6,4},{8,6},{10,8},{12,10},{14,12},{16,14},{18,... | collective-permute-start | bytes 6144008 | tf_op jit(solution)/shard_map/ppermute | solution.py:19
  579.3 50.1 %collective-permute-start.23 = (f32[20,80,160]{2,1,0:T(8,128)}, f32[20,80,160]{2,1,0:T(8,128)S(1)}, u32[]{:S(2)}, u32[]{:S(2)}) collective-permute-start(f32[20,80,160]{2,1,0:T(8,128)} %get-tuple-element.70), channel_id=1, source_target_pairs={{0,1},{1,0},{2,3},{3,2},{4,5},{5,4},{6,7},{7,6},{8,9},{9,8},{10,11... | collective-permute-start | bytes 3072008 | tf_op jit(solution)/shard_map/ppermute | solution.py:19
  595.5 91.7 %collective-permute-start.30 = (f32[20,160,160]{2,1,0:T(8,128)}, f32[20,160,160]{2,1,0:T(8,128)S(1)}, u32[]{:S(2)}, u32[]{:S(2)}) collective-permute-start(f32[20,160,160]{2,1,0:T(8,128)} %get-tuple-element.82), channel_id=1, source_target_pairs={{0,30},{2,0},{4,2},{6,4},{8,6},{10,8},{12,10},{14,12},{16,14},{18,... | collective-permute-start | bytes 6144008 | tf_op jit(solution)/shard_map/ppermute | solution.py:19
  630.6 33.2 %collective-permute-start.26 = (f32[20,80,160]{2,1,0:T(8,128)}, f32[20,80,160]{2,1,0:T(8,128)}, u32[]{:S(2)}, u32[]{:S(2)}) collective-permute-start(f32[20,80,160]{2,1,0:T(8,128)} %get-tuple-element.75), channel_id=1, source_target_pairs={{0,1},{1,0},{2,3},{3,2},{4,5},{5,4},{6,7},{7,6},{8,9},{9,8},{10,11... | collective-permute-start | bytes 3072008 | tf_op jit(solution)/shard_map/ppermute | solution.py:19
  631.8 67.1 %collective-permute-start.29 = (f32[20,80,160]{2,1,0:T(8,128)}, f32[20,80,160]{2,1,0:T(8,128)}, u32[]{:S(2)}, u32[]{:S(2)}) collective-permute-start(f32[20,80,160]{2,1,0:T(8,128)} %get-tuple-element.80), channel_id=1, source_target_pairs={{0,1},{1,0},{2,3},{3,2},{4,5},{5,4},{6,7},{7,6},{8,9},{9,8},{10,11... | collective-permute-start | bytes 3072008 | tf_op jit(solution)/shard_map/ppermute | solution.py:19
  643.0 72.4 %collective-permute-start.20 = (f32[20,160,160]{2,1,0:T(8,128)}, f32[20,160,160]{2,1,0:T(8,128)}, u32[]{:S(2)}, u32[]{:S(2)}) collective-permute-start(f32[20,160,160]{2,1,0:T(8,128)} %get-tuple-element.68), channel_id=1, source_target_pairs={{0,30},{2,0},{4,2},{6,4},{8,6},{10,8},{12,10},{14,12},{16,14},{18,... | collective-permute-start | bytes 6144008 | tf_op jit(solution)/shard_map/ppermute | solution.py:19
  660.8 89.7 %collective-permute-start.25 = (f32[20,160,160]{2,1,0:T(8,128)}, f32[20,160,160]{2,1,0:T(8,128)}, u32[]{:S(2)}, u32[]{:S(2)}) collective-permute-start(f32[20,160,160]{2,1,0:T(8,128)} %get-tuple-element.74), channel_id=1, source_target_pairs={{0,30},{2,0},{4,2},{6,4},{8,6},{10,8},{12,10},{14,12},{16,14},{18,... | collective-permute-start | bytes 6144008 | tf_op jit(solution)/shard_map/ppermute | solution.py:19
  675.1 110.4 %collective-permute-start.28 = (f32[20,160,160]{2,1,0:T(8,128)}, f32[20,160,160]{2,1,0:T(8,128)S(1)}, u32[]{:S(2)}, u32[]{:S(2)}) collective-permute-start(f32[20,160,160]{2,1,0:T(8,128)} %get-tuple-element.79), channel_id=1, source_target_pairs={{0,30},{2,0},{4,2},{6,4},{8,6},{10,8},{12,10},{14,12},{16,14},{18,... | collective-permute-start | bytes 6144008 | tf_op jit(solution)/shard_map/ppermute | solution.py:19
  706.7 114.0 %collective-permute-start.31 = (f32[20,160,160]{2,1,0:T(8,128)S(1)}, f32[20,160,160]{2,1,0:T(8,128)S(1)}, u32[]{:S(2)}, u32[]{:S(2)}) collective-permute-start(f32[20,160,160]{2,1,0:T(8,128)S(1)} %get-tuple-element.84), channel_id=1, source_target_pairs={{0,30},{2,0},{4,2},{6,4},{8,6},{10,8},{12,10},{14,12},{16,14},{18,... | collective-permute-start | bytes 6144008 | tf_op jit(solution)/shard_map/ppermute | solution.py:19
  (46 other events, 684.4 us)
